TPU v7x, 512 devices: a whole 4x8x8 slice. The times are simulated.
512 devices in a mesh: grp: 16 (over z, core), lev: 32 (over y, x).
Axes of the slice: x: 4, y: 8, z: 8, core: 2. Of those that a mesh axis runs over, the one named last changes fastest.
Arguments:
- ocean_field: bfloat16 [16, 64, 524288], P(None, 'lev', 'grp'), may hold values from -6 to 6
- climatology: float32 [64, 524288], P(None, ('grp', 'lev')), may hold values from -3 to 3
- land_mask: int32 [524288], P(('grp', 'lev')), may hold values 0 or 1
- bottom_index: int32 [524288], P(('grp', 'lev')), may hold values from 16 to 64
- vertical_modes: bfloat16 [16, 64], replicated, may hold values from -0.75 to 0.75
Outputs:
- factor: float32 [256, 256], replicated
- whitened: float32 [256, 524288], P(None, ('grp', 'lev'))
All inputs are finite; a program needn't handle non-finite values. No bound on the sum of `land_mask` on one device may be relied on, other than what follows from the above.
Results may differ from a plain program's by a relative error of at most 0.008.
Values may be sent and summed in bfloat16 or wider, within the bound.
A program may use at most 128 MiB of HBM per device.

v0:
```python
import jax
import jax.numpy as jnp
from jax import lax
from jax.sharding import PartitionSpec as P


def on_device(ocean_field, climatology, land_mask, bottom_index, vertical_modes):
    levels = vertical_modes.shape[1]
    col_dev = climatology.shape[1]
    level_ids = lax.broadcasted_iota(jnp.int32, (levels, col_dev), 0)
    water = jnp.where(
        (level_ids < bottom_index[None, :]) & (land_mask[None, :] == 1), 1.0, 0.0
    ).astype(jnp.float32)
    anomaly = (
        (
            lax.all_to_all(ocean_field, "lev", split_axis=2, concat_axis=1, tiled=True).astype(
                jnp.float32
            )
            - climatology[None]
        )
        * water[None]
    ).astype(jnp.bfloat16)
    coefficients = jnp.einsum(
        "ml,dlc->dmc", vertical_modes, anomaly, preferred_element_type=jnp.float32
    )
    width = coefficients.shape[0] * coefficients.shape[1]
    stacked = coefficients.reshape(width, col_dev)
    total_cols = col_dev * lax.axis_size("grp") * lax.axis_size("lev")
    gram_local = jnp.dot(stacked, stacked.T, precision=lax.Precision.HIGHEST) / jnp.float32(
        total_cols
    )
    gram = lax.psum(gram_local, ("grp", "lev"))
    factor = jnp.linalg.cholesky(gram).T
    whitened = jax.scipy.linalg.solve_triangular(factor.T, stacked, lower=True)
    return (factor, whitened)


def solution(mesh):
    in_specs = (
        P(None, "lev", "grp"),
        P(None, ("grp", "lev")),
        P(("grp", "lev")),
        P(("grp", "lev")),
        P(),
    )
    out_specs = (P(), P(None, ("grp", "lev")))
    return jax.shard_map(
        on_device, mesh=mesh, in_specs=in_specs, out_specs=out_specs, check_vma=False
    )
```

profile of v0, /device:TPU:1, one launch (start us, length us, event | category | flops | bytes accessed | tf_op | source)
XLA Modules:
  0.0 543.6 jit_solution(2691613196666592210)
XLA Ops:
  7.2 32.4 %copy.16 = bf16[16,2,32768]{0,1,2:T(2,128)(2,1)} copy(bf16[16,2,32768]{2,1,0:T(2,128)(2,1)} %param.5) | data formatting | bytes 4194304 | tf_op args[0]
  39.6 20.8 %reshape.93 = bf16[32,2,16384]{2,1,0:T(2,128)(2,1)} reshape(bf16[32768,2,16]{2,1,0:T(2,128)(2,1)} %bitcast.51) | data formatting | bytes 4194304
  60.4 10.6 %all-to-all-start = ((bf16[32,2,16384]{2,1,0:T(2,128)(2,1)}), bf16[32,2,16384]{2,1,0:T(2,128)(2,1)S(1)}, u32[]{:S(2)}, u32[]{:S(2)}) async-start(bf16[32,2,16384]{2,1,0:T(2,128)(2,1)} %reshape.93), calls=%async_computation | async-start | bytes 4194304 | tf_op jit(solution)/shard_map/all_to_all | solution.py:16
  71.2 48.3 %all-to-all-done = bf16[32,2,16384]{2,1,0:T(2,128)(2,1)S(1)} async-done(((bf16[32,2,16384]{2,1,0:T(2,128)(2,1)}), bf16[32,2,16384]{2,1,0:T(2,128)(2,1)S(1)}, u32[]{:S(2)}, u32[]{:S(2)}) %all-to-all-start) | async-done | bytes 2097184 | tf_op jit(solution)/shard_map/all_to_all | solution.py:16
  119.5 14.3 %reshape.94 = bf16[32768,2,16]{2,1,0:T(2,128)(2,1)} reshape(bf16[32,2,16384]{2,1,0:T(2,128)(2,1)S(1)} %all-to-all-done) | data formatting | bytes 4194304
  133.8 17.5 %convert_bitcast_fusion = f32[16,32,2,1024]{0,2,3,1:T(2,128)} fusion(bf16[16,2,32,1024]{0,1,3,2:T(2,128)(2,1)} %bitcast.50), kind=kLoop, calls=%fused_computation.2 | loop fusion | flops 1048576 | bytes 6291456 | tf_op jit(solution)/shard_map/convert_element_type | solution.py:16
  151.3 39.0 %copy.17 = f32[16,32,2,1024]{3,2,1,0:T(2,128)} copy(f32[16,32,2,1024]{0,2,3,1:T(2,128)} %convert_bitcast_fusion) | data formatting | bytes 8388608 | tf_op jit(solution)/shard_map/convert_element_type | solution.py:16
  190.3 6.1 %reshape.90 = f32[16,64,1024]{2,1,0:T(8,128)} reshape(f32[16,32,2,1024]{3,2,1,0:T(2,128)} %copy.17) | data formatting | bytes 8388608 | tf_op jit(solution)/shard_map/convert_element_type | solution.py:16
  196.3 3.0 fusion
  199.3 1.7 convolution_multiply_fusion
  201.1 0.1 fusion.16
  201.2 270.0 %all-reduce.3.cloned.1.call-done = f32[256,256]{0,1:T(8,128)} async-done(((f32[256,256]{0,1:T(8,128)}), f32[256,256]{0,1:T(8,128)}) %all-reduce.3.cloned.1.call-update) | async-done | bytes 262160 | tf_op jit(solution)/shard_map/psum | solution.py:32
  471.2 1.1 copy.19
  472.3 1.0 fusion.3
  473.3 11.7 %cholesky.50 = f32[128,128]{1,0:T(8,128)S(1)} custom-call(f32[128,128]{1,0:T(8,128)S(1)} %cholesky.118), custom_call_target="Cholesky" | custom-call | tf_op jit(solution)/shard_map/jit(cholesky)/cholesky | solution.py:33
  485.1 9.8 %custom-call.15 = f32[1,128,128]{1,2,0:T(8,128)S(1)} custom-call(f32[1,128,128]{2,1,0:T(8,128)S(1)} %get-tuple-element.33), custom_call_target="InvertDiagBlocksLowerTriangular" | custom-call | tf_op jit(solution)/shard_map/jit(cholesky)/cholesky | solution.py:33
  494.9 0.2 constant_dynamic-update-slice_fusion.1
  495.1 0.3 convolution_subtract_fusion.1
  495.4 11.7 %cholesky.105 = f32[128,128]{1,0:T(8,128)S(1)} custom-call(f32[128,128]{1,0:T(8,128)S(1)} %convolution_subtract_fusion.1), custom_call_target="Cholesky" | custom-call | tf_op jit(solution)/shard_map/jit(cholesky)/cholesky | solution.py:33
  507.1 0.6 compare_reduce_fusion
  509.1 0.1 triangular_solve.46
  509.2 4.2 while.1
  509.4 0.6 fusion.25
  510.0 1.4 bitcast_dynamic-update-slice_fusion.2
  511.4 0.6 fusion.25
  512.0 1.4 bitcast_dynamic-update-slice_fusion.2
  513.4 19.7 %custom-call.16 = f32[2,128,128]{1,2,0:T(8,128)S(1)} custom-call(f32[2,128,128]{2,1,0:T(8,128)S(1)} %get-tuple-element.9), custom_call_target="InvertDiagBlocksLowerTriangular" | custom-call | tf_op jit(solution)/shard_map/jit(_solve_triangular)/triangular_solve | solution.py:34
  533.1 0.6 fusion.10
  533.7 0.6 convolution_subtract_fusion
  534.3 0.6 fusion.9
  534.9 1.0 pad_maximum_fusion
  536.0 0.8 copy.20
  (21 shorter events, 0.3 us)
Async XLA Ops:
  7.2 189.2 %copy-start = (bf16[16,64]{1,0:T(8,128)(2,1)S(1)}, bf16[16,64]{1,0:T(8,128)(2,1)}, u32[]{:S(2)}) copy-start(bf16[16,64]{1,0:T(8,128)(2,1)} %param.9) | copy-start | bytes 6148
  60.4 10.7 %copy-start.3 = (s32[1024]{0:T(1024)S(1)}, s32[1024]{0:T(1024)}, u32[]{:S(2)}) copy-start(s32[1024]{0:T(1024)} %param.7) | copy-start | bytes 12292
  60.4 10.7 %copy-start.2 = (s32[1024]{0:T(1024)S(1)}, s32[1024]{0:T(1024)}, u32[]{:S(2)}) copy-start(s32[1024]{0:T(1024)} %param.8) | copy-start | bytes 12292
  60.4 59.1 %all-to-all-start = ((bf16[32,2,16384]{2,1,0:T(2,128)(2,1)}), bf16[32,2,16384]{2,1,0:T(2,128)(2,1)S(1)}, u32[]{:S(2)}, u32[]{:S(2)}) async-start(bf16[32,2,16384]{2,1,0:T(2,128)(2,1)} %reshape.93), calls=%async_computation | async-start | bytes 4194304 | tf_op jit(solution)/shard_map/all_to_all | solution.py:16
  71.0 400.2 %all-reduce.3.cloned.1.call-start = ((), (), s32[]{:S(2)}) async-start(), calls=%async_computation.1 | async-start | bytes 524288 | tf_op jit(solution)/shard_map/psum | solution.py:32
  190.3 6.1 %copy-start.1 = (f32[64,1024]{1,0:T(8,128)S(1)}, f32[64,1024]{1,0:T(8,128)}, u32[]{:S(2)}) copy-start(f32[64,1024]{1,0:T(8,128)} %param.6) | copy-start | bytes 786436
Sparse Core Ops, SparseCore 0:
  201.2 269.9 all-reduce.2
where the time goes:
time: 549 us; the launch traced here: 544 us
  waiting for transfers between devices  318 us (58%)
  local copies, waits for them, and re-layouts  119 us (22%)
  other arithmetic  73.3 us (13%)
  between operations  15.5 us (3%)
  starting transfers between devices  10.7 us (2%)
  matrix products  7.03 us (1%)
    psum x1, waiting for transfers between devices, on_device(): gram = lax.psum(gram_local, ('grp', 'lev'))  270 us
    unnamed x12, local copies, waits for them, and re-layouts  68.3 us
    all_to_all x1, waiting for transfers between devices, on_device(): lax.all_to_all(ocean_field, 'lev', split_axis=2, concat_axis=1, tiled=True)  48.3 us
    convert_element_type x2, local copies, waits for them, and re-layouts, on_device(): lax.all_to_all(ocean_field, 'lev', split_axis=2, concat_axis=1, tiled=True)  45.1 us
    another operation x6, other arithmetic, on_device(): factor = jnp.linalg.cholesky(gram).T  34 us
    another operation x4, other arithmetic, on_device(): whitened = jax.scipy.linalg.solve_triangular(factor.T, stacked, lower=True)  20.8 us
    convert_element_type x1, other arithmetic, on_device(): lax.all_to_all(ocean_field, 'lev', split_axis=2, concat_axis=1, tiled=True)  17.5 us
  transfers between devices with their start and end apart: 2, of which 2 were waited for; matrix products, arithmetic and copies ran while one was open for 0% of the time, Pallas kernels for 0%

commit v1 on v0

v1 whole, which is shorter than its diff:
```python
import functools

import jax
import jax.numpy as jnp
from jax import lax
from jax.experimental import pallas as pl
from jax.experimental.pallas import tpu as pltpu
from jax.sharding import PartitionSpec as P

MESH = pl.DeviceIdType.MESH
DAYS = 16
MODES = 16
LANES = 128


def exchange_kernel(
    n_grp, n_lev, total_cols,
    ocean_ref, clim_ref, mask_ref, bottom_ref, modes_ref,
    stacked_ref, gram_ref,
    recv, clim_rows, limit_rows, weights, anomaly, part, rs_buf, sum_buf, gather_buf,
    local_sem, a_send, a_recv, r_send, r_recv, s_send, s_recv, g_send, g_recv,
):
    me_g = lax.axis_index("grp")
    me_l = lax.axis_index("lev")
    slabs = clim_ref.shape[1] // LANES
    rows = 2 * slabs

    def lev_peer(o):
        return lax.rem(me_l + o, n_lev)

    def lev_from(o):
        return lax.rem(me_l + n_lev - o, n_lev)

    def grp_peer(o):
        return lax.rem(me_g + o, n_grp)

    def grp_from(o):
        return lax.rem(me_g + n_grp - o, n_grp)

    barrier = pltpu.get_barrier_semaphore()

    @pl.loop(1, n_lev)
    def _(o):
        pl.semaphore_signal(barrier, inc=1, device_id=(me_g, lev_peer(o)), device_id_type=MESH)

    @pl.loop(1, n_grp)
    def _(o):
        pl.semaphore_signal(barrier, inc=1, device_id=(grp_peer(o), me_l), device_id_type=MESH)

    pl.semaphore_wait(barrier, n_lev + n_grp - 2)

    def block_copy(to, slot, k):
        return pltpu.make_async_remote_copy(
            src_ref=ocean_ref.at[:, pl.ds(pl.multiple_of(to * rows, rows), rows), :],
            dst_ref=recv.at[slot],
            send_sem=a_send.at[k],
            recv_sem=a_recv.at[k],
            device_id=(me_g, to),
            device_id_type=MESH,
        )

    @pl.loop(1, n_lev)
    def _(o):
        block_copy(lev_peer(o), me_l, o).start()

    own = pltpu.make_async_copy(
        ocean_ref.at[:, pl.ds(pl.multiple_of(me_l * rows, rows), rows), :], recv.at[me_l], local_sem
    )
    own.start()

    limit = jnp.where(mask_ref[...] == 1, bottom_ref[...], 0)
    for slab in range(slabs):
        limit_rows[2 * slab : 2 * slab + 1, :] = limit[slab : slab + 1, :]
        limit_rows[2 * slab + 1 : 2 * slab + 2, :] = limit[slab : slab + 1, :] - 1

    @pl.loop(0, clim_ref.shape[0] // 8)
    def _(t):
        block = clim_ref[pl.ds(pl.multiple_of(t * 8, 8), 8), :]
        for k in range(8):
            for slab in range(slabs):
                row = 2 * slab + k % 2
                clim_rows[4 * t + k // 2, row : row + 1, :] = block[
                    k : k + 1, slab * LANES : (slab + 1) * LANES
                ]

    width = slabs * MODES
    depth = n_lev * rows
    levels = modes_ref.shape[1]
    r = lax.broadcasted_iota(jnp.int32, (width, MODES), 0)
    m = lax.broadcasted_iota(jnp.int32, (width, MODES), 1)
    spread_modes = jnp.where(lax.rem(r, MODES) == m, 1.0, 0.0).astype(jnp.bfloat16)
    l = lax.broadcasted_iota(jnp.int32, (levels, depth), 0)
    q = lax.broadcasted_iota(jnp.int32, (levels, depth), 1)
    spread_levels = jnp.where(2 * (q // rows) + lax.rem(q, 2) == l, 1.0, 0.0).astype(jnp.bfloat16)
    tall = jnp.dot(spread_modes, modes_ref[...], preferred_element_type=jnp.float32).astype(jnp.bfloat16)
    wide = jnp.dot(tall, spread_levels, preferred_element_type=jnp.float32)
    r = lax.broadcasted_iota(jnp.int32, (width, depth), 0)
    q = lax.broadcasted_iota(jnp.int32, (width, depth), 1)
    weights[...] = jnp.where(r // MODES == lax.rem(q, rows) // 2, wide, 0.0).astype(jnp.bfloat16)

    def use(s):
        water = limit_rows[...] > 2 * s
        clim = clim_rows[s]
        for d in range(DAYS):
            diff = recv[s, d].astype(jnp.float32) - clim
            anomaly[pl.ds(pl.multiple_of(s * rows, rows), rows), d * LANES : (d + 1) * LANES] = jnp.where(
                water, diff, 0.0
            ).astype(jnp.bfloat16)

    own.wait()
    use(me_l)

    @pl.loop(1, n_lev)
    def _(o):
        s = lev_from(o)
        block_copy(s, s, o).wait_recv()
        use(s)

    coef = jnp.dot(weights[...], anomaly[...], preferred_element_type=jnp.float32)
    for d in range(DAYS):
        for slab in range(slabs):
            stacked_ref[d * MODES : (d + 1) * MODES, slab * LANES : (slab + 1) * LANES] = coef[
                slab * MODES : (slab + 1) * MODES, d * LANES : (d + 1) * LANES
            ]
    stacked = stacked_ref[...]
    part[...] = lax.dot_general(
        stacked, stacked, (((1,), (1,)), ((), ())),
        precision=lax.Precision.HIGHEST, preferred_element_type=jnp.float32,
    )

    piece = part.shape[0] // n_lev

    def rows_of(i):
        return pl.ds(pl.multiple_of(i * piece, piece), piece)

    def scatter_copy(to, slot, k):
        return pltpu.make_async_remote_copy(
            src_ref=part.at[rows_of(to)], dst_ref=rs_buf.at[slot],
            send_sem=r_send.at[k], recv_sem=r_recv.at[k],
            device_id=(me_g, to), device_id_type=MESH,
        )

    @pl.loop(1, n_lev)
    def _(o):
        scatter_copy(lev_peer(o), me_l, o).start()

    rs_buf[me_l] = part[rows_of(me_l)]

    @pl.loop(1, n_lev)
    def _(o):
        s = lev_from(o)
        scatter_copy(s, s, o).wait_recv()

    sum_buf[me_g] = jnp.sum(rs_buf[...], axis=0)

    def sum_copy(to, slot, k):
        return pltpu.make_async_remote_copy(
            src_ref=sum_buf.at[me_g], dst_ref=sum_buf.at[slot],
            send_sem=s_send.at[k], recv_sem=s_recv.at[k],
            device_id=(to, me_l), device_id_type=MESH,
        )

    @pl.loop(1, n_grp)
    def _(o):
        sum_copy(grp_peer(o), me_g, o).start()

    @pl.loop(1, n_grp)
    def _(o):
        s = grp_from(o)
        sum_copy(s, s, o).wait_recv()

    gather_buf[me_l] = jnp.sum(sum_buf[...], axis=0) * (1.0 / total_cols)

    def gather_copy(to, slot, k):
        return pltpu.make_async_remote_copy(
            src_ref=gather_buf.at[me_l], dst_ref=gather_buf.at[slot],
            send_sem=g_send.at[k], recv_sem=g_recv.at[k],
            device_id=(me_g, to), device_id_type=MESH,
        )

    @pl.loop(1, n_lev)
    def _(o):
        gather_copy(lev_peer(o), me_l, o).start()

    gram_ref[rows_of(me_l)] = gather_buf[me_l]

    @pl.loop(1, n_lev)
    def _(o):
        s = lev_from(o)
        gather_copy(s, s, o).wait_recv()
        gram_ref[rows_of(s)] = gather_buf[s]

    @pl.loop(1, n_lev)
    def _(o):
        block_copy(lev_peer(o), me_l, o).wait_send()
        scatter_copy(lev_peer(o), me_l, o).wait_send()
        gather_copy(lev_peer(o), me_l, o).wait_send()

    @pl.loop(1, n_grp)
    def _(o):
        sum_copy(grp_peer(o), me_g, o).wait_send()


def exchange(n_grp, n_lev, ocean, climatology, land_mask, bottom_index, modes):
    days, levels_dev, cols_grp = ocean.shape
    col_dev = climatology.shape[1]
    slabs = col_dev // LANES
    rows = levels_dev * slabs
    total_cols = col_dev * n_grp * n_lev
    width = DAYS * MODES
    piece = width // n_lev
    tiles = cols_grp // LANES
    ocean = ocean.reshape(days, levels_dev, tiles, LANES).transpose(0, 2, 1, 3)
    ocean = ocean.reshape(days, tiles * levels_dev, LANES)
    vmem = pl.BlockSpec(memory_space=pltpu.VMEM)
    return pl.pallas_call(
        functools.partial(exchange_kernel, n_grp, n_lev, total_cols),
        out_shape=(
            jax.ShapeDtypeStruct((width, col_dev), jnp.float32),
            jax.ShapeDtypeStruct((width, width), jnp.float32),
        ),
        in_specs=[pl.BlockSpec(memory_space=pl.ANY)] + [vmem] * 4,
        out_specs=(vmem, vmem),
        scratch_shapes=[
            pltpu.VMEM((n_lev, days, rows, LANES), jnp.bfloat16),
            pltpu.VMEM((n_lev, rows, LANES), jnp.float32),
            pltpu.VMEM((rows, LANES), jnp.int32),
            pltpu.VMEM((slabs * MODES, n_lev * rows), jnp.bfloat16),
            pltpu.VMEM((n_lev * rows, days * LANES), jnp.bfloat16),
            pltpu.VMEM((width, width), jnp.float32),
            pltpu.VMEM((n_lev, piece, width), jnp.float32),
            pltpu.VMEM((n_grp, piece, width), jnp.float32),
            pltpu.VMEM((n_lev, piece, width), jnp.float32),
            pltpu.SemaphoreType.DMA,
        ]
        + [pltpu.SemaphoreType.DMA((n_lev,))] * 4
        + [pltpu.SemaphoreType.DMA((n_grp,))] * 2
        + [pltpu.SemaphoreType.DMA((n_lev,))] * 2,
        compiler_params=pltpu.CompilerParams(
            collective_id=0, has_side_effects=True, vmem_limit_bytes=40 * 1024 * 1024
        ),
        name="exchange",
    )(
        ocean, climatology,
        land_mask.reshape(slabs, LANES), bottom_index.reshape(slabs, LANES), modes,
    )


def mm(a, b, dims=((1,), (0,))):
    return lax.dot_general(a, b, (dims, ((), ())), precision=lax.Precision.HIGHEST, preferred_element_type=jnp.float32)


def eliminate(a):
    n = a.shape[0]
    w = 8
    lane = lax.broadcasted_iota(jnp.int32, (w, n), 1)
    sub = lax.broadcasted_iota(jnp.int32, (w, n), 0)
    rows = [a[w * h : w * h + w] for h in range(n // w)]

    def spread(x):
        return jnp.broadcast_to(x, (w, n))

    for g in range(n // w):
        at = g * w
        col = [spread(rows[g][:, at + k : at + k + 1]) for k in range(w)]
        row = rows[g]
        pivots, splats = [], []
        for k in range(w):
            inv = 1.0 / spread(col[k][k : k + 1])
            pivot = jnp.where(lane == at + k, inv, spread(row[k : k + 1]) * inv)
            pivots.append(jnp.where((lane > at + k) & (lane < at + w), 0.0, pivot))
            splats.append({j: spread(col[j][k : k + 1]) * inv for j in range(k + 1, w)})
            if k < w - 1:
                m = jnp.where(sub > k, col[k], 0.0)
                row = jnp.where((lane == at + k) & (sub > k), 0.0, row) - m * pivot
                for j in range(k + 1, w):
                    col[j] = col[j] - m * splats[k][j]
        rows[g] = row
        inside = (lane >= at) & (lane < at + w)
        for h in range(g + 1, n // w):
            c = [spread(rows[h][:, at + k : at + k + 1]) for k in range(w)]
            out = jnp.where(inside, 0.0, rows[h])
            for k in range(w):
                for j in range(k + 1, w):
                    c[j] = c[j] - c[k] * splats[k][j]
            for k in range(w):
                out = out - c[k] * pivots[k]
            rows[h] = out
    upper, inverse = [], []
    for h in range(n // w):
        at = sub + w * h
        scale = lax.rsqrt(spread(jnp.sum(jnp.where(lane == at, rows[h], 0.0), axis=1, keepdims=True)))
        upper.append(jnp.where(lane >= at, rows[h] * scale, 0.0))
        inverse.append(jnp.where(lane == at, scale, jnp.where(lane < at, rows[h] * scale, 0.0)))
    return jnp.concatenate(upper, axis=0), jnp.concatenate(inverse, axis=0)

def whiten_kernel(gram_ref, stacked_ref, factor_ref, whitened_ref):
    half = gram_ref.shape[0] // 2
    r11, i11 = eliminate(gram_ref[:half, :half])
    r12 = mm(i11, gram_ref[:half, half:])
    factor_ref[:half, :half] = r11
    factor_ref[:half, half:] = r12
    factor_ref[half:, :half] = jnp.zeros((half, half), jnp.float32)
    rest = gram_ref[half:, half:] - mm(r12, r12, ((0,), (0,)))
    first = mm(i11, stacked_ref[:half])
    whitened_ref[:half] = first
    left = stacked_ref[half:] - mm(r12, first, ((0,), (0,)))
    r22, i22 = eliminate(rest)
    factor_ref[half:, half:] = r22
    whitened_ref[half:] = mm(i22, left)


def whiten(gram, stacked):
    vmem = pl.BlockSpec(memory_space=pltpu.VMEM)
    return pl.pallas_call(
        whiten_kernel,
        out_shape=(
            jax.ShapeDtypeStruct(gram.shape, jnp.float32),
            jax.ShapeDtypeStruct(stacked.shape, jnp.float32),
        ),
        in_specs=[vmem, vmem],
        out_specs=(vmem, vmem),
        compiler_params=pltpu.CompilerParams(vmem_limit_bytes=40 * 1024 * 1024),
        name="whiten",
    )(gram, stacked)


def solution(mesh):
    n_grp, n_lev = mesh.shape["grp"], mesh.shape["lev"]

    def on_device(ocean_field, climatology, land_mask, bottom_index, vertical_modes):
        stacked, gram = exchange(
            n_grp, n_lev, ocean_field, climatology, land_mask, bottom_index, vertical_modes
        )
        return whiten(gram, stacked)

    in_specs = (
        P(None, "lev", "grp"),
        P(None, ("grp", "lev")),
        P(("grp", "lev")),
        P(("grp", "lev")),
        P(),
    )
    out_specs = (P(), P(None, ("grp", "lev")))
    return jax.shard_map(
        on_device, mesh=mesh, in_specs=in_specs, out_specs=out_specs, check_vma=False
    )
```

time: 549 us -> 111 us (0.20)
  waiting for transfers between devices: 318 us -> 0 us
  local copies, waits for them, and re-layouts: 119 us -> 4.59 us
  Pallas kernels: 0 us -> 106 us
  other arithmetic: 73.3 us -> 0 us
  between operations: 15.5 us -> 0.65 us
  starting transfers between devices: 10.7 us -> 0 us
  matrix products: 7.03 us -> 0 us
    psum x1 -> x0, waiting for transfers between devices: 270 us -> none  [on_device(): gram = lax.psum(gram_local, ('grp', 'lev'))]
    pallas_call x0 -> x2, Pallas kernels: none -> 106 us  [the longest x1 95.4 us: exchange(): pl.pallas_call(functools.partial(exchange_kernel, n_grp, n_lev, total_col...]
    unnamed x12 -> x10, local copies, waits for them, and re-layouts: 68.3 us -> 4.59 us
    another operation x10 -> x0, other arithmetic: 54.7 us -> none  [the longest x6 34 us: on_device(): factor = jnp.linalg.cholesky(gram).T]
    all_to_all x1 -> x0, waiting for transfers between devices: 48.3 us -> none  [on_device(): lax.all_to_all(ocean_field, 'lev', split_axis=2, concat_axis=1, tiled=True)]
    convert_element_type x2 -> x0, local copies, waits for them, and re-layouts: 45.1 us -> none  [on_device(): lax.all_to_all(ocean_field, 'lev', split_axis=2, concat_axis=1, tiled=True)]
    convert_element_type x1 -> x0, other arithmetic: 17.5 us -> none  [on_device(): lax.all_to_all(ocean_field, 'lev', split_axis=2, concat_axis=1, tiled=True)]
    all_to_all x1 -> x0, starting transfers between devices: 10.6 us -> none  [on_device(): lax.all_to_all(ocean_field, 'lev', split_axis=2, concat_axis=1, tiled=True)]
  transfers between devices with their start and end apart: 2 -> 0, of which waited for: 2 -> 0; matrix products, arithmetic and copies ran while one was open for 0% -> 0% of each run, Pallas kernels for 0% -> 0%
where the time goes in v1:
time: 111 us
  Pallas kernels  106 us (95%)
  local copies, waits for them, and re-layouts  4.59 us (4%)
    pallas_call x1, Pallas kernels, exchange(): pl.pallas_call(functools.partial(exchange_kernel, n_grp, n_lev, total_col...  95.4 us
    pallas_call x1, Pallas kernels, whiten(): pl.pallas_call(whiten_kernel, out_shape=(jax.ShapeDtypeStruct(gram.shape,...  10.4 us
    unnamed x10, local copies, waits for them, and re-layouts  4.59 us

profile of v1, /device:TPU:1, one launch (start us, length us, event | category | flops | bytes accessed | tf_op | source)
XLA Modules:
  0.0 111.0 jit_solution(12964823713594671701)
XLA Ops:
  0.6 0.0 copy-start
  0.6 1.6 %copy-done = bf16[16,2,32768]{2,1,0:T(2,128)(2,1)S(1)} copy-done((bf16[16,2,32768]{2,1,0:T(2,128)(2,1)S(1)}, bf16[16,2,32768]{2,1,0:T(2,128)(2,1)}, u32[]{:S(2)}) %copy-start) | copy-done | bytes 2097176
  2.2 0.0 copy-start.1
  2.2 0.9 copy-done.1
  3.2 0.0 copy-start.2
  3.2 0.7 copy-done.2
  3.9 0.0 copy-start.3
  3.9 0.7 copy-done.3
  4.5 0.0 copy-start.4
  4.6 0.7 copy-done.4
  5.2 95.4 %exchange.1 = (f32[256,1024]{1,0:T(8,128)S(1)}, f32[256,256]{1,0:T(8,128)S(1)}) custom-call(bf16[16,512,128]{2,1,0:T(8,128)(2,1)S(1)} %bitcast.7, f32[64,1024]{1,0:T(8,128)S(1)} %copy-done.1, s32[8,128]{1,0:T(8,128)S(1)} %bitcast.8, s32[8,128]{1,0:T(8,128)S(1)} %bitcast.9, bf16[16,64]{1,0:T(8,128)(2,1)S(1)} %copy-done.4), custom_call_target="tpu_custom_call" | custom-call | tf_op jit(solution)/shard_map/exchange/pallas_call | solution.py:216
  100.7 10.4 %whiten.1 = (f32[256,256]{1,0:T(8,128)}, f32[256,1024]{1,0:T(8,128)}) custom-call(f32[256,256]{1,0:T(8,128)S(1)} %get-tuple-element.4.gram_ref, f32[256,1024]{1,0:T(8,128)S(1)} %get-tuple-element.5.stacked_ref), custom_call_target="tpu_custom_call" | custom-call | tf_op jit(solution)/shard_map/whiten/pallas_call | solution.py:315
Async XLA Ops:
  0.6 1.6 %copy-start = (bf16[16,2,32768]{2,1,0:T(2,128)(2,1)S(1)}, bf16[16,2,32768]{2,1,0:T(2,128)(2,1)}, u32[]{:S(2)}) copy-start(bf16[16,2,32768]{2,1,0:T(2,128)(2,1)} %param.5) | copy-start | bytes 6291460
  2.2 0.9 copy-start.1
  3.2 0.7 copy-start.2
  3.9 0.7 copy-start.3
  4.5 0.7 copy-start.4

commit v2 on v1

--- a/solution.py
+++ b/solution.py
@@ -11,43 +11,75 @@
 DAYS = 16
 MODES = 16
 LANES = 128
+VMEM_BYTES = 60 * 1024 * 1024
+CORES = 2
+N_X = 4
 
 
 def exchange_kernel(
-    n_grp, n_lev, total_cols,
-    ocean_ref, clim_ref, mask_ref, bottom_ref, modes_ref,
-    stacked_ref, gram_ref,
-    recv, clim_rows, limit_rows, weights, anomaly, part, rs_buf, sum_buf, gather_buf,
-    local_sem, a_send, a_recv, r_send, r_recv, s_send, s_recv, g_send, g_recv,
+    n_grp, n_lev,
+    ocean_ref, clim_hbm, mask_hbm, bottom_hbm, modes_hbm,
+    stacked_hbm, gram_ref,
+    clim_ref, mask_ref, bottom_ref, modes_ref,
+    stacked_ref, recv, clim_rows, limit_rows, weights, anomaly, packed, pair_buf, rs_buf, sum_buf, gather_buf,
+    in_sem, local_sem, out_sem, a_send, a_recv, p_sem, r_send, r_recv, s_send, s_recv, g_send, g_recv,
 ):
     me_g = lax.axis_index("grp")
     me_l = lax.axis_index("lev")
+    core = lax.rem(me_g, CORES)
+    me_z = me_g // CORES
+    n_z = n_grp // CORES
+    n_y = n_lev // N_X
     slabs = clim_ref.shape[1] // LANES
     rows = 2 * slabs
 
-    def lev_peer(o):
-        return lax.rem(me_l + o, n_lev)
+    inputs = [
+        pltpu.make_async_copy(src, dst, in_sem.at[i])
+        for i, (src, dst) in enumerate(
+            [(mask_hbm, mask_ref), (bottom_hbm, bottom_ref), (modes_hbm, modes_ref), (clim_hbm, clim_ref)]
+        )
+    ]
+    for copy in inputs:
+        copy.start()
+
+    def spiral(i, n):
+        half = (i + 1) // 2
+        return lax.rem(n // 2 + jnp.where(lax.rem(i, 2) == 1, n - half, half), n)
+
+    def lev_at(o, sign):
+        dy, dx = spiral(o // N_X, n_y), spiral(lax.rem(o, N_X), N_X)
+        y = lax.rem(me_l // N_X + n_y + sign * dy, n_y)
+        x = lax.rem(lax.rem(me_l, N_X) + N_X + sign * dx, N_X)
+        return y * N_X + x
+
+    def lev_to(o):
+        return lev_at(o, 1)
 
     def lev_from(o):
-        return lax.rem(me_l + n_lev - o, n_lev)
-
-    def grp_peer(o):
-        return lax.rem(me_g + o, n_grp)
-
-    def grp_from(o):
-        return lax.rem(me_g + n_grp - o, n_grp)
+        return lev_at(o, -1)
+
+    def z_to(o):
+        return lax.rem(me_z + o, n_z)
+
+    def z_from(o):
+        return lax.rem(me_z + n_z - o, n_z)
+
+    partner = (me_z * CORES + 1 - core, me_l)
 
     barrier = pltpu.get_barrier_semaphore()
 
-    @pl.loop(1, n_lev)
-    def _(o):
-        pl.semaphore_signal(barrier, inc=1, device_id=(me_g, lev_peer(o)), device_id_type=MESH)
-
-    @pl.loop(1, n_grp)
-    def _(o):
-        pl.semaphore_signal(barrier, inc=1, device_id=(grp_peer(o), me_l), device_id_type=MESH)
-
-    pl.semaphore_wait(barrier, n_lev + n_grp - 2)
+    @pl.loop(0, n_lev - 1)
+    def _(o):
+        pl.semaphore_signal(barrier, inc=1, device_id=(me_g, lev_to(o)), device_id_type=MESH)
+
+    @pl.loop(1, n_z)
+    def _(o):
+        pl.semaphore_signal(
+            barrier, inc=1, device_id=(z_to(o) * CORES + core, me_l), device_id_type=MESH
+        )
+
+    pl.semaphore_signal(barrier, inc=1, device_id=partner, device_id_type=MESH)
+    pl.semaphore_wait(barrier, n_lev + n_z - 1)
 
     def block_copy(to, slot, k):
         return pltpu.make_async_remote_copy(
@@ -59,14 +91,16 @@
             device_id_type=MESH,
         )
 
-    @pl.loop(1, n_lev)
-    def _(o):
-        block_copy(lev_peer(o), me_l, o).start()
+    @pl.loop(0, n_lev - 1)
+    def _(o):
+        block_copy(lev_to(o), me_l, o).start()
 
     own = pltpu.make_async_copy(
         ocean_ref.at[:, pl.ds(pl.multiple_of(me_l * rows, rows), rows), :], recv.at[me_l], local_sem
     )
     own.start()
+    for copy in inputs:
+        copy.wait()
 
     limit = jnp.where(mask_ref[...] == 1, bottom_ref[...], 0)
     for slab in range(slabs):
@@ -110,7 +144,7 @@
     own.wait()
     use(me_l)
 
-    @pl.loop(1, n_lev)
+    @pl.loop(0, n_lev - 1)
     def _(o):
         s = lev_from(o)
         block_copy(s, s, o).wait_recv()
@@ -122,83 +156,113 @@
             stacked_ref[d * MODES : (d + 1) * MODES, slab * LANES : (slab + 1) * LANES] = coef[
                 slab * MODES : (slab + 1) * MODES, d * LANES : (d + 1) * LANES
             ]
-    stacked = stacked_ref[...]
-    part[...] = lax.dot_general(
-        stacked, stacked, (((1,), (1,)), ((), ())),
-        precision=lax.Precision.HIGHEST, preferred_element_type=jnp.float32,
-    )
-
-    piece = part.shape[0] // n_lev
-
-    def rows_of(i):
-        return pl.ds(pl.multiple_of(i * piece, piece), piece)
+
+    keep = pltpu.make_async_copy(stacked_ref, stacked_hbm, out_sem)
+    keep.start()
+
+    half = stacked_ref.shape[0] // 2
+    top, low = stacked_ref[:half], stacked_ref[half:]
+    long, short = half // n_lev, half // CORES // n_lev
+
+    def gram_block(x, y):
+        return lax.dot_general(
+            x, y, (((1,), (1,)), ((), ())),
+            precision=lax.Precision.HIGHEST, preferred_element_type=jnp.float32,
+        )
+
+    last = gram_block(low, low)
+    for c, first in enumerate((gram_block(top, top), gram_block(top, low))):
+        for i in range(n_lev):
+            packed[c, i, :long] = first[i * long : (i + 1) * long]
+            at = c * (half // CORES) + i * short
+            packed[c, i, long:] = last[at : at + short]
+
+    def pair_copy(src, dst, k):
+        return pltpu.make_async_remote_copy(
+            src_ref=src, dst_ref=dst, send_sem=p_sem.at[k, 0], recv_sem=p_sem.at[k, 1],
+            device_id=partner, device_id_type=MESH,
+        )
+
+    to_pair = pair_copy(packed.at[1 - core], pair_buf, 0)
+    to_pair.start()
+    to_pair.wait()
+    packed[core] = packed[core] + pair_buf[...]
 
     def scatter_copy(to, slot, k):
         return pltpu.make_async_remote_copy(
-            src_ref=part.at[rows_of(to)], dst_ref=rs_buf.at[slot],
+            src_ref=packed.at[core, to], dst_ref=rs_buf.at[slot],
             send_sem=r_send.at[k], recv_sem=r_recv.at[k],
             device_id=(me_g, to), device_id_type=MESH,
         )
 
-    @pl.loop(1, n_lev)
-    def _(o):
-        scatter_copy(lev_peer(o), me_l, o).start()
-
-    rs_buf[me_l] = part[rows_of(me_l)]
-
-    @pl.loop(1, n_lev)
+    @pl.loop(0, n_lev - 1)
+    def _(o):
+        scatter_copy(lev_to(o), me_l, o).start()
+
+    rs_buf[me_l] = packed[core, me_l]
+
+    @pl.loop(0, n_lev - 1)
     def _(o):
         s = lev_from(o)
         scatter_copy(s, s, o).wait_recv()
 
-    sum_buf[me_g] = jnp.sum(rs_buf[...], axis=0)
+    sum_buf[me_z] = jnp.sum(rs_buf[...], axis=0)
 
     def sum_copy(to, slot, k):
         return pltpu.make_async_remote_copy(
-            src_ref=sum_buf.at[me_g], dst_ref=sum_buf.at[slot],
+            src_ref=sum_buf.at[me_z], dst_ref=sum_buf.at[slot],
             send_sem=s_send.at[k], recv_sem=s_recv.at[k],
-            device_id=(to, me_l), device_id_type=MESH,
-        )
-
-    @pl.loop(1, n_grp)
-    def _(o):
-        sum_copy(grp_peer(o), me_g, o).start()
-
-    @pl.loop(1, n_grp)
-    def _(o):
-        s = grp_from(o)
+            device_id=(to * CORES + core, me_l), device_id_type=MESH,
+        )
+
+    @pl.loop(1, n_z)
+    def _(o):
+        sum_copy(z_to(o), me_z, o).start()
+
+    @pl.loop(1, n_z)
+    def _(o):
+        s = z_from(o)
         sum_copy(s, s, o).wait_recv()
 
-    gather_buf[me_l] = jnp.sum(sum_buf[...], axis=0) * (1.0 / total_cols)
+    total_cols = clim_ref.shape[1] * n_grp * n_lev
+    gather_buf[core, me_l] = jnp.sum(sum_buf[...], axis=0) * (1.0 / total_cols)
 
     def gather_copy(to, slot, k):
         return pltpu.make_async_remote_copy(
-            src_ref=gather_buf.at[me_l], dst_ref=gather_buf.at[slot],
+            src_ref=gather_buf.at[core, me_l], dst_ref=gather_buf.at[core, slot],
             send_sem=g_send.at[k], recv_sem=g_recv.at[k],
             device_id=(me_g, to), device_id_type=MESH,
         )
 
-    @pl.loop(1, n_lev)
-    def _(o):
-        gather_copy(lev_peer(o), me_l, o).start()
-
-    gram_ref[rows_of(me_l)] = gather_buf[me_l]
-
-    @pl.loop(1, n_lev)
+    @pl.loop(0, n_lev - 1)
+    def _(o):
+        gather_copy(lev_to(o), me_l, o).start()
+
+    @pl.loop(0, n_lev - 1)
     def _(o):
         s = lev_from(o)
         gather_copy(s, s, o).wait_recv()
-        gram_ref[rows_of(s)] = gather_buf[s]
-
-    @pl.loop(1, n_lev)
-    def _(o):
-        block_copy(lev_peer(o), me_l, o).wait_send()
-        scatter_copy(lev_peer(o), me_l, o).wait_send()
-        gather_copy(lev_peer(o), me_l, o).wait_send()
-
-    @pl.loop(1, n_grp)
-    def _(o):
-        sum_copy(grp_peer(o), me_g, o).wait_send()
+
+    to_pair = pair_copy(gather_buf.at[core], gather_buf.at[core], 1)
+    to_pair.start()
+    to_pair.wait()
+    for c in range(CORES):
+        for i in range(n_lev):
+            gram_ref[c, i * long : (i + 1) * long] = gather_buf[c, i, :long]
+            at = c * (half // CORES) + i * short
+            gram_ref[CORES, at : at + short] = gather_buf[c, i, long:]
+
+    keep.wait()
+
+    @pl.loop(0, n_lev - 1)
+    def _(o):
+        block_copy(lev_to(o), me_l, o).wait_send()
+        scatter_copy(lev_to(o), me_l, o).wait_send()
+        gather_copy(lev_to(o), me_l, o).wait_send()
+
+    @pl.loop(1, n_z)
+    def _(o):
+        sum_copy(z_to(o), me_z, o).wait_send()
 
 
 def exchange(n_grp, n_lev, ocean, climatology, land_mask, bottom_index, modes):
@@ -206,44 +270,59 @@
     col_dev = climatology.shape[1]
     slabs = col_dev // LANES
     rows = levels_dev * slabs
-    total_cols = col_dev * n_grp * n_lev
     width = DAYS * MODES
-    piece = width // n_lev
+    half = width // 2
+    piece = (half + half // CORES) // n_lev
     tiles = cols_grp // LANES
     ocean = ocean.reshape(days, levels_dev, tiles, LANES).transpose(0, 2, 1, 3)
     ocean = ocean.reshape(days, tiles * levels_dev, LANES)
     vmem = pl.BlockSpec(memory_space=pltpu.VMEM)
+    operands = (
+        ocean, climatology,
+        land_mask.reshape(slabs, LANES), bottom_index.reshape(slabs, LANES), modes,
+    )
     return pl.pallas_call(
-        functools.partial(exchange_kernel, n_grp, n_lev, total_cols),
+        functools.partial(exchange_kernel, n_grp, n_lev),
         out_shape=(
             jax.ShapeDtypeStruct((width, col_dev), jnp.float32),
-            jax.ShapeDtypeStruct((width, width), jnp.float32),
+            jax.ShapeDtypeStruct((CORES + 1, half, half), jnp.float32),
         ),
-        in_specs=[pl.BlockSpec(memory_space=pl.ANY)] + [vmem] * 4,
-        out_specs=(vmem, vmem),
+        in_specs=[pl.BlockSpec(memory_space=pltpu.HBM)] * 5,
+        out_specs=(pl.BlockSpec(memory_space=pltpu.HBM), vmem),
         scratch_shapes=[
+            pltpu.VMEM(climatology.shape, jnp.float32),
+            pltpu.VMEM((slabs, LANES), jnp.int32),
+            pltpu.VMEM((slabs, LANES), jnp.int32),
+            pltpu.VMEM(modes.shape, jnp.bfloat16),
+            pltpu.VMEM((width, col_dev), jnp.float32),
             pltpu.VMEM((n_lev, days, rows, LANES), jnp.bfloat16),
             pltpu.VMEM((n_lev, rows, LANES), jnp.float32),
             pltpu.VMEM((rows, LANES), jnp.int32),
             pltpu.VMEM((slabs * MODES, n_lev * rows), jnp.bfloat16),
             pltpu.VMEM((n_lev * rows, days * LANES), jnp.bfloat16),
-            pltpu.VMEM((width, width), jnp.float32),
-            pltpu.VMEM((n_lev, piece, width), jnp.float32),
-            pltpu.VMEM((n_grp, piece, width), jnp.float32),
-            pltpu.VMEM((n_lev, piece, width), jnp.float32),
+            pltpu.VMEM((CORES, n_lev, piece, half), jnp.float32),
+            pltpu.VMEM((n_lev, piece, half), jnp.float32),
+            pltpu.VMEM((n_lev, piece, half), jnp.float32),
+            pltpu.VMEM((n_grp // CORES, piece, half), jnp.float32),
+            pltpu.VMEM((CORES, n_lev, piece, half), jnp.float32),
+            pltpu.SemaphoreType.DMA((4,)),
             pltpu.SemaphoreType.DMA,
-        ]
-        + [pltpu.SemaphoreType.DMA((n_lev,))] * 4
-        + [pltpu.SemaphoreType.DMA((n_grp,))] * 2
-        + [pltpu.SemaphoreType.DMA((n_lev,))] * 2,
+            pltpu.SemaphoreType.DMA,
+            pltpu.SemaphoreType.DMA((n_lev,)),
+            pltpu.SemaphoreType.DMA((n_lev,)),
+            pltpu.SemaphoreType.DMA((2, 2)),
+            pltpu.SemaphoreType.DMA((n_lev,)),
+            pltpu.SemaphoreType.DMA((n_lev,)),
+            pltpu.SemaphoreType.DMA((n_grp // CORES,)),
+            pltpu.SemaphoreType.DMA((n_grp // CORES,)),
+            pltpu.SemaphoreType.DMA((n_lev,)),
+            pltpu.SemaphoreType.DMA((n_lev,)),
+        ],
         compiler_params=pltpu.CompilerParams(
-            collective_id=0, has_side_effects=True, vmem_limit_bytes=40 * 1024 * 1024
+            collective_id=0, has_side_effects=True, vmem_limit_bytes=VMEM_BYTES
         ),
         name="exchange",
-    )(
-        ocean, climatology,
-        land_mask.reshape(slabs, LANES), bottom_index.reshape(slabs, LANES), modes,
-    )
+    )(*operands)
 
 
 def mm(a, b, dims=((1,), (0,))):
@@ -294,33 +373,59 @@
         inverse.append(jnp.where(lane == at, scale, jnp.where(lane < at, rows[h] * scale, 0.0)))
     return jnp.concatenate(upper, axis=0), jnp.concatenate(inverse, axis=0)
 
-def whiten_kernel(gram_ref, stacked_ref, factor_ref, whitened_ref):
-    half = gram_ref.shape[0] // 2
-    r11, i11 = eliminate(gram_ref[:half, :half])
-    r12 = mm(i11, gram_ref[:half, half:])
+def whiten_kernel(
+    gram_hbm, stacked_hbm, factor_hbm, whitened_hbm,
+    gram_ref, stacked_ref, factor_ref, whitened_ref, sem,
+):
+    half = gram_ref.shape[1]
+    gram_in = pltpu.make_async_copy(gram_hbm, gram_ref, sem.at[0])
+    stacked_in = pltpu.make_async_copy(stacked_hbm, stacked_ref, sem.at[1])
+    first_out = pltpu.make_async_copy(whitened_ref.at[:half], whitened_hbm.at[:half], sem.at[2])
+    second_out = pltpu.make_async_copy(whitened_ref.at[half:], whitened_hbm.at[half:], sem.at[3])
+    factor_out = pltpu.make_async_copy(factor_ref, factor_hbm, sem.at[4])
+    gram_in.start()
+    stacked_in.start()
+    gram_in.wait()
+    r11, i11 = eliminate(gram_ref[0])
+    r12 = mm(i11, gram_ref[1])
     factor_ref[:half, :half] = r11
     factor_ref[:half, half:] = r12
     factor_ref[half:, :half] = jnp.zeros((half, half), jnp.float32)
-    rest = gram_ref[half:, half:] - mm(r12, r12, ((0,), (0,)))
+    rest = gram_ref[2] - mm(r12, r12, ((0,), (0,)))
+    stacked_in.wait()
     first = mm(i11, stacked_ref[:half])
     whitened_ref[:half] = first
+    first_out.start()
     left = stacked_ref[half:] - mm(r12, first, ((0,), (0,)))
     r22, i22 = eliminate(rest)
     factor_ref[half:, half:] = r22
+    factor_out.start()
     whitened_ref[half:] = mm(i22, left)
+    second_out.start()
+    first_out.wait()
+    factor_out.wait()
+    second_out.wait()
 
 
 def whiten(gram, stacked):
-    vmem = pl.BlockSpec(memory_space=pltpu.VMEM)
+    hbm = pl.BlockSpec(memory_space=pltpu.HBM)
+    factor_shape = (stacked.shape[0],) * 2
     return pl.pallas_call(
         whiten_kernel,
         out_shape=(
-            jax.ShapeDtypeStruct(gram.shape, jnp.float32),
+            jax.ShapeDtypeStruct(factor_shape, jnp.float32),
             jax.ShapeDtypeStruct(stacked.shape, jnp.float32),
         ),
-        in_specs=[vmem, vmem],
-        out_specs=(vmem, vmem),
-        compiler_params=pltpu.CompilerParams(vmem_limit_bytes=40 * 1024 * 1024),
+        in_specs=[hbm, hbm],
+        out_specs=(hbm, hbm),
+        scratch_shapes=[
+            pltpu.VMEM(gram.shape, jnp.float32),
+            pltpu.VMEM(stacked.shape, jnp.float32),
+            pltpu.VMEM(factor_shape, jnp.float32),
+            pltpu.VMEM(stacked.shape, jnp.float32),
+            pltpu.SemaphoreType.DMA((5,)),
+        ],
+        compiler_params=pltpu.CompilerParams(vmem_limit_bytes=VMEM_BYTES),
         name="whiten",
     )(gram, stacked)
 

time: 111 us -> 101 us (0.910)
  Pallas kernels: 106 us -> 101 us
  local copies, waits for them, and re-layouts: 4.59 us -> 0 us
    pallas_call x2, Pallas kernels: 106 us -> 101 us  [the longest x1 89.3 us: exchange(): pl.pallas_call(functools.partial(exchange_kernel, n_grp, n_lev), out_shap...]
    unnamed x10 -> x0, local copies, waits for them, and re-layouts: 4.59 us -> none
where the time goes in v2:
time: 101 us
  Pallas kernels  101 us (100%)
    pallas_call x1, Pallas kernels, exchange(): pl.pallas_call(functools.partial(exchange_kernel, n_grp, n_lev), out_shap...  89.3 us
    pallas_call x1, Pallas kernels, whiten(): pl.pallas_call(whiten_kernel, out_shape=(jax.ShapeDtypeStruct(factor_shap...  11.3 us

profile of v2, /device:TPU:1, one launch (start us, length us, event | category | flops | bytes accessed | tf_op | source)
XLA Modules:
  0.0 101.2 jit_solution(12512311571902293615)
XLA Ops:
  0.6 89.3 %exchange.1 = (f32[256,1024]{1,0:T(8,128)}, f32[3,128,128]{2,1,0:T(8,128)}) custom-call(bf16[16,512,128]{2,1,0:T(8,128)(2,1)} %bitcast.7, f32[64,1024]{1,0:T(8,128)} %clim_hbm.1, s32[8,128]{1,0:T(8,128)} %bitcast.8, s32[8,128]{1,0:T(8,128)} %bitcast.9, bf16[16,64]{1,0:T(8,128)(2,1)} %modes_hbm.1), custom_call_target="tpu_custom_call" | custom-call | tf_op jit(solution)/shard_map/exchange/pallas_call | solution.py:284
  90.0 11.3 %whiten.1 = (f32[256,256]{1,0:T(8,128)}, f32[256,1024]{1,0:T(8,128)}) custom-call(f32[3,128,128]{2,1,0:T(8,128)} %get-tuple-element.4.gram_hbm, f32[256,1024]{1,0:T(8,128)} %get-tuple-element.5.stacked_hbm), custom_call_target="tpu_custom_call" | custom-call | tf_op jit(solution)/shard_map/whiten/pallas_call | solution.py:413

commit v3 on v2

--- a/solution.py
+++ b/solution.py
@@ -19,9 +19,9 @@
 def exchange_kernel(
     n_grp, n_lev,
     ocean_ref, clim_hbm, mask_hbm, bottom_hbm, modes_hbm,
-    stacked_hbm, gram_ref,
+    stacked_hbm, gram_hbm,
     clim_ref, mask_ref, bottom_ref, modes_ref,
-    stacked_ref, recv, clim_rows, limit_rows, weights, anomaly, packed, pair_buf, rs_buf, sum_buf, gather_buf,
+    stacked_ref, recv, clim_rows, limit_rows, weights, anomaly, theirs, packed, pair_buf, rs_buf, sum_buf, gather_buf,
     in_sem, local_sem, out_sem, a_send, a_recv, p_sem, r_send, r_recv, s_send, s_recv, g_send, g_recv,
 ):
     me_g = lax.axis_index("grp")
@@ -42,21 +42,23 @@
     for copy in inputs:
         copy.start()
 
+    def far_first(n):
+        return sorted(range(n), key=lambda d: -min(d, n - d))
+
+    y_at = [lax.rem(me_l // N_X + d, n_y) * N_X for d in range(n_y)]
+    x_at = [lax.rem(lax.rem(me_l, N_X) + d, N_X) for d in range(N_X)]
+    steps = [(dy, dx) for dy in far_first(n_y) for dx in far_first(N_X)][:-1]
+    peers = [y_at[dy] + x_at[dx] for dy, dx in steps]
+    senders = [y_at[-dy % n_y] + x_at[-dx % N_X] for dy, dx in steps]
+
     def spiral(i, n):
         half = (i + 1) // 2
-        return lax.rem(n // 2 + jnp.where(lax.rem(i, 2) == 1, n - half, half), n)
-
-    def lev_at(o, sign):
-        dy, dx = spiral(o // N_X, n_y), spiral(lax.rem(o, N_X), N_X)
-        y = lax.rem(me_l // N_X + n_y + sign * dy, n_y)
-        x = lax.rem(lax.rem(me_l, N_X) + N_X + sign * dx, N_X)
+        return lax.rem(n // 2 + jnp.where(lax.rem(i, 2) == 1, half, n - half), n)
+
+    def sender(o):
+        y = lax.rem(me_l // N_X + spiral(o // N_X, n_y), n_y)
+        x = lax.rem(lax.rem(me_l, N_X) + spiral(lax.rem(o, N_X), N_X), N_X)
         return y * N_X + x
-
-    def lev_to(o):
-        return lev_at(o, 1)
-
-    def lev_from(o):
-        return lev_at(o, -1)
 
     def z_to(o):
         return lax.rem(me_z + o, n_z)
@@ -68,12 +70,9 @@
 
     barrier = pltpu.get_barrier_semaphore()
 
-    @pl.loop(0, n_lev - 1)
-    def _(o):
-        pl.semaphore_signal(barrier, inc=1, device_id=(me_g, lev_to(o)), device_id_type=MESH)
-
-    @pl.loop(1, n_z)
-    def _(o):
+    for peer in peers:
+        pl.semaphore_signal(barrier, inc=1, device_id=(me_g, peer), device_id_type=MESH)
+    for o in range(1, n_z):
         pl.semaphore_signal(
             barrier, inc=1, device_id=(z_to(o) * CORES + core, me_l), device_id_type=MESH
         )
@@ -91,9 +90,8 @@
             device_id_type=MESH,
         )
 
-    @pl.loop(0, n_lev - 1)
-    def _(o):
-        block_copy(lev_to(o), me_l, o).start()
+    for o, peer in enumerate(peers):
+        block_copy(peer, me_l, o).start()
 
     own = pltpu.make_async_copy(
         ocean_ref.at[:, pl.ds(pl.multiple_of(me_l * rows, rows), rows), :], recv.at[me_l], local_sem
@@ -146,7 +144,7 @@
 
     @pl.loop(0, n_lev - 1)
     def _(o):
-        s = lev_from(o)
+        s = sender(o)
         block_copy(s, s, o).wait_recv()
         use(s)
 
@@ -157,12 +155,12 @@
                 slab * MODES : (slab + 1) * MODES, d * LANES : (d + 1) * LANES
             ]
 
-    keep = pltpu.make_async_copy(stacked_ref, stacked_hbm, out_sem)
+    keep = pltpu.make_async_copy(stacked_ref, stacked_hbm, out_sem.at[0])
     keep.start()
 
     half = stacked_ref.shape[0] // 2
-    top, low = stacked_ref[:half], stacked_ref[half:]
-    long, short = half // n_lev, half // CORES // n_lev
+    share = half // CORES
+    long, short = half // n_lev, share // n_lev
 
     def gram_block(x, y):
         return lax.dot_general(
@@ -170,12 +168,13 @@
             precision=lax.Precision.HIGHEST, preferred_element_type=jnp.float32,
         )
 
-    last = gram_block(low, low)
-    for c, first in enumerate((gram_block(top, top), gram_block(top, low))):
+    def pack(c, out):
+        row, rest = pl.multiple_of(c * half, half), pl.multiple_of(half + c * share, share)
+        first = gram_block(stacked_ref[:half], stacked_ref[pl.ds(row, half)])
+        last = gram_block(stacked_ref[pl.ds(rest, share)], stacked_ref[half:])
         for i in range(n_lev):
-            packed[c, i, :long] = first[i * long : (i + 1) * long]
-            at = c * (half // CORES) + i * short
-            packed[c, i, long:] = last[at : at + short]
+            out[i, :long] = first[i * long : (i + 1) * long]
+            out[i, long:] = last[i * short : (i + 1) * short]
 
     def pair_copy(src, dst, k):
         return pltpu.make_async_remote_copy(
@@ -183,27 +182,26 @@
             device_id=partner, device_id_type=MESH,
         )
 
-    to_pair = pair_copy(packed.at[1 - core], pair_buf, 0)
+    pack(1 - core, theirs)
+    to_pair = pair_copy(theirs, pair_buf, 0)
     to_pair.start()
+    pack(core, packed)
     to_pair.wait()
-    packed[core] = packed[core] + pair_buf[...]
+    packed[...] = packed[...] + pair_buf[...]
 
     def scatter_copy(to, slot, k):
         return pltpu.make_async_remote_copy(
-            src_ref=packed.at[core, to], dst_ref=rs_buf.at[slot],
+            src_ref=packed.at[to], dst_ref=rs_buf.at[slot],
             send_sem=r_send.at[k], recv_sem=r_recv.at[k],
             device_id=(me_g, to), device_id_type=MESH,
         )
 
-    @pl.loop(0, n_lev - 1)
-    def _(o):
-        scatter_copy(lev_to(o), me_l, o).start()
-
-    rs_buf[me_l] = packed[core, me_l]
-
-    @pl.loop(0, n_lev - 1)
-    def _(o):
-        s = lev_from(o)
+    for o, peer in enumerate(peers):
+        scatter_copy(peer, me_l, o).start()
+
+    rs_buf[me_l] = packed[me_l]
+
+    for o, s in enumerate(senders):
         scatter_copy(s, s, o).wait_recv()
 
     sum_buf[me_z] = jnp.sum(rs_buf[...], axis=0)
@@ -215,12 +213,9 @@
             device_id=(to * CORES + core, me_l), device_id_type=MESH,
         )
 
-    @pl.loop(1, n_z)
-    def _(o):
+    for o in range(1, n_z):
         sum_copy(z_to(o), me_z, o).start()
-
-    @pl.loop(1, n_z)
-    def _(o):
+    for o in range(1, n_z):
         s = z_from(o)
         sum_copy(s, s, o).wait_recv()
 
@@ -234,35 +229,27 @@
             device_id=(me_g, to), device_id_type=MESH,
         )
 
-    @pl.loop(0, n_lev - 1)
-    def _(o):
-        gather_copy(lev_to(o), me_l, o).start()
-
-    @pl.loop(0, n_lev - 1)
-    def _(o):
-        s = lev_from(o)
+    for o, peer in enumerate(peers):
+        gather_copy(peer, me_l, o).start()
+    for o, s in enumerate(senders):
         gather_copy(s, s, o).wait_recv()
 
     to_pair = pair_copy(gather_buf.at[core], gather_buf.at[core], 1)
     to_pair.start()
+    mine = pltpu.make_async_copy(gather_buf.at[core], gram_hbm.at[core], out_sem.at[1])
+    mine.start()
     to_pair.wait()
-    for c in range(CORES):
-        for i in range(n_lev):
-            gram_ref[c, i * long : (i + 1) * long] = gather_buf[c, i, :long]
-            at = c * (half // CORES) + i * short
-            gram_ref[CORES, at : at + short] = gather_buf[c, i, long:]
-
+    other = pltpu.make_async_copy(gather_buf.at[1 - core], gram_hbm.at[1 - core], out_sem.at[2])
+    other.start()
+    for o, peer in enumerate(peers):
+        block_copy(peer, me_l, o).wait_send()
+        scatter_copy(peer, me_l, o).wait_send()
+        gather_copy(peer, me_l, o).wait_send()
+    for o in range(1, n_z):
+        sum_copy(z_to(o), me_z, o).wait_send()
     keep.wait()
-
-    @pl.loop(0, n_lev - 1)
-    def _(o):
-        block_copy(lev_to(o), me_l, o).wait_send()
-        scatter_copy(lev_to(o), me_l, o).wait_send()
-        gather_copy(lev_to(o), me_l, o).wait_send()
-
-    @pl.loop(1, n_z)
-    def _(o):
-        sum_copy(z_to(o), me_z, o).wait_send()
+    mine.wait()
+    other.wait()
 
 
 def exchange(n_grp, n_lev, ocean, climatology, land_mask, bottom_index, modes):
@@ -276,7 +263,7 @@
     tiles = cols_grp // LANES
     ocean = ocean.reshape(days, levels_dev, tiles, LANES).transpose(0, 2, 1, 3)
     ocean = ocean.reshape(days, tiles * levels_dev, LANES)
-    vmem = pl.BlockSpec(memory_space=pltpu.VMEM)
+    hbm = pl.BlockSpec(memory_space=pltpu.HBM)
     operands = (
         ocean, climatology,
         land_mask.reshape(slabs, LANES), bottom_index.reshape(slabs, LANES), modes,
@@ -285,10 +272,10 @@
         functools.partial(exchange_kernel, n_grp, n_lev),
         out_shape=(
             jax.ShapeDtypeStruct((width, col_dev), jnp.float32),
-            jax.ShapeDtypeStruct((CORES + 1, half, half), jnp.float32),
+            jax.ShapeDtypeStruct((CORES, n_lev, piece, half), jnp.float32),
         ),
-        in_specs=[pl.BlockSpec(memory_space=pltpu.HBM)] * 5,
-        out_specs=(pl.BlockSpec(memory_space=pltpu.HBM), vmem),
+        in_specs=[hbm] * 5,
+        out_specs=(hbm, hbm),
         scratch_shapes=[
             pltpu.VMEM(climatology.shape, jnp.float32),
             pltpu.VMEM((slabs, LANES), jnp.int32),
@@ -300,14 +287,15 @@
             pltpu.VMEM((rows, LANES), jnp.int32),
             pltpu.VMEM((slabs * MODES, n_lev * rows), jnp.bfloat16),
             pltpu.VMEM((n_lev * rows, days * LANES), jnp.bfloat16),
-            pltpu.VMEM((CORES, n_lev, piece, half), jnp.float32),
+            pltpu.VMEM((n_lev, piece, half), jnp.float32),
+            pltpu.VMEM((n_lev, piece, half), jnp.float32),
             pltpu.VMEM((n_lev, piece, half), jnp.float32),
             pltpu.VMEM((n_lev, piece, half), jnp.float32),
             pltpu.VMEM((n_grp // CORES, piece, half), jnp.float32),
             pltpu.VMEM((CORES, n_lev, piece, half), jnp.float32),
             pltpu.SemaphoreType.DMA((4,)),
             pltpu.SemaphoreType.DMA,
-            pltpu.SemaphoreType.DMA,
+            pltpu.SemaphoreType.DMA((3,)),
             pltpu.SemaphoreType.DMA((n_lev,)),
             pltpu.SemaphoreType.DMA((n_lev,)),
             pltpu.SemaphoreType.DMA((2, 2)),
@@ -375,10 +363,11 @@
 
 def whiten_kernel(
     gram_hbm, stacked_hbm, factor_hbm, whitened_hbm,
-    gram_ref, stacked_ref, factor_ref, whitened_ref, sem,
+    pieces, gram_ref, stacked_ref, factor_ref, whitened_ref, sem,
 ):
     half = gram_ref.shape[1]
-    gram_in = pltpu.make_async_copy(gram_hbm, gram_ref, sem.at[0])
+    long, short = half // pieces.shape[1], half // CORES // pieces.shape[1]
+    gram_in = pltpu.make_async_copy(gram_hbm, pieces, sem.at[0])
     stacked_in = pltpu.make_async_copy(stacked_hbm, stacked_ref, sem.at[1])
     first_out = pltpu.make_async_copy(whitened_ref.at[:half], whitened_hbm.at[:half], sem.at[2])
     second_out = pltpu.make_async_copy(whitened_ref.at[half:], whitened_hbm.at[half:], sem.at[3])
@@ -386,6 +375,11 @@
     gram_in.start()
     stacked_in.start()
     gram_in.wait()
+    for c in range(CORES):
+        for i in range(pieces.shape[1]):
+            gram_ref[c, i * long : (i + 1) * long] = pieces[c, i, :long]
+            at = c * (half // CORES) + i * short
+            gram_ref[CORES, at : at + short] = pieces[c, i, long:]
     r11, i11 = eliminate(gram_ref[0])
     r12 = mm(i11, gram_ref[1])
     factor_ref[:half, :half] = r11
@@ -420,6 +414,7 @@
         out_specs=(hbm, hbm),
         scratch_shapes=[
             pltpu.VMEM(gram.shape, jnp.float32),
+            pltpu.VMEM((CORES + 1, gram.shape[3], gram.shape[3]), jnp.float32),
             pltpu.VMEM(stacked.shape, jnp.float32),
             pltpu.VMEM(factor_shape, jnp.float32),
             pltpu.VMEM(stacked.shape, jnp.float32),

time: 101 us -> 99.7 us (0.987)
  Pallas kernels: 101 us -> 98.9 us
    pallas_call x1, Pallas kernels: 89.3 us -> 87.6 us  [exchange(): pl.pallas_call(functools.partial(exchange_kernel, n_grp, n_lev), out_shap...]
where the time goes in v3:
time: 99.7 us; the launch traced here: 99.5 us
  Pallas kernels  98.9 us (99%)
    pallas_call x1, Pallas kernels, exchange(): pl.pallas_call(functools.partial(exchange_kernel, n_grp, n_lev), out_shap...  87.6 us
    pallas_call x1, Pallas kernels, whiten(): pl.pallas_call(whiten_kernel, out_shape=(jax.ShapeDtypeStruct(factor_shap...  11.3 us

profile of v3, /device:TPU:1, one launch (start us, length us, event | category | flops | bytes accessed | tf_op | source)
XLA Modules:
  0.0 99.5 jit_solution(502887159835383127)
XLA Ops:
  0.6 87.6 %exchange.1 = (f32[256,1024]{1,0:T(8,128)}, f32[2,32,6,128]{3,2,1,0:T(8,128)}) custom-call(bf16[16,512,128]{2,1,0:T(8,128)(2,1)} %bitcast.7, f32[64,1024]{1,0:T(8,128)} %clim_hbm.1, s32[8,128]{1,0:T(8,128)} %bitcast.8, s32[8,128]{1,0:T(8,128)} %bitcast.9, bf16[16,64]{1,0:T(8,128)(2,1)} %modes_hbm.1), custom_call_target="tpu_custom_call" | custom-call | tf_op jit(solution)/shard_map/exchange/pallas_call | solution.py:271
  88.3 11.3 %whiten.1 = (f32[256,256]{1,0:T(8,128)}, f32[256,1024]{1,0:T(8,128)}) custom-call(f32[2,32,6,128]{3,2,1,0:T(8,128)} %get-tuple-element.4.gram_hbm, f32[256,1024]{1,0:T(8,128)} %get-tuple-element.5.stacked_hbm), custom_call_target="tpu_custom_call" | custom-call | tf_op jit(solution)/shard_map/whiten/pallas_call | solution.py:407

commit v4 on v3

--- a/solution.py
+++ b/solution.py
@@ -11,7 +11,7 @@
 DAYS = 16
 MODES = 16
 LANES = 128
-VMEM_BYTES = 60 * 1024 * 1024
+VMEM_BYTES = 40 * 1024 * 1024
 CORES = 2
 N_X = 4
 
@@ -19,10 +19,10 @@
 def exchange_kernel(
     n_grp, n_lev,
     ocean_ref, clim_hbm, mask_hbm, bottom_hbm, modes_hbm,
-    stacked_hbm, gram_hbm,
+    stacked_ref, gram_ref,
     clim_ref, mask_ref, bottom_ref, modes_ref,
-    stacked_ref, recv, clim_rows, limit_rows, weights, anomaly, theirs, packed, pair_buf, rs_buf, sum_buf, gather_buf,
-    in_sem, local_sem, out_sem, a_send, a_recv, p_sem, r_send, r_recv, s_send, s_recv, g_send, g_recv,
+    recv, clim_rows, limit_rows, weights, anomaly, theirs, packed, pair_buf, rs_buf, sum_buf, gather_buf,
+    in_sem, local_sem, a_send, a_recv, p_sem, r_send, r_recv, s_send, s_recv, g_send, g_recv,
 ):
     me_g = lax.axis_index("grp")
     me_l = lax.axis_index("lev")
@@ -155,9 +155,6 @@
                 slab * MODES : (slab + 1) * MODES, d * LANES : (d + 1) * LANES
             ]
 
-    keep = pltpu.make_async_copy(stacked_ref, stacked_hbm, out_sem.at[0])
-    keep.start()
-
     half = stacked_ref.shape[0] // 2
     share = half // CORES
     long, short = half // n_lev, share // n_lev
@@ -236,20 +233,15 @@
 
     to_pair = pair_copy(gather_buf.at[core], gather_buf.at[core], 1)
     to_pair.start()
-    mine = pltpu.make_async_copy(gather_buf.at[core], gram_hbm.at[core], out_sem.at[1])
-    mine.start()
+    gram_ref[core] = gather_buf[core]
     to_pair.wait()
-    other = pltpu.make_async_copy(gather_buf.at[1 - core], gram_hbm.at[1 - core], out_sem.at[2])
-    other.start()
+    gram_ref[1 - core] = gather_buf[1 - core]
     for o, peer in enumerate(peers):
         block_copy(peer, me_l, o).wait_send()
         scatter_copy(peer, me_l, o).wait_send()
         gather_copy(peer, me_l, o).wait_send()
     for o in range(1, n_z):
         sum_copy(z_to(o), me_z, o).wait_send()
-    keep.wait()
-    mine.wait()
-    other.wait()
 
 
 def exchange(n_grp, n_lev, ocean, climatology, land_mask, bottom_index, modes):
@@ -263,11 +255,12 @@
     tiles = cols_grp // LANES
     ocean = ocean.reshape(days, levels_dev, tiles, LANES).transpose(0, 2, 1, 3)
     ocean = ocean.reshape(days, tiles * levels_dev, LANES)
-    hbm = pl.BlockSpec(memory_space=pltpu.HBM)
+    vmem, hbm = pl.BlockSpec(memory_space=pltpu.VMEM), pl.BlockSpec(memory_space=pltpu.HBM)
     operands = (
         ocean, climatology,
         land_mask.reshape(slabs, LANES), bottom_index.reshape(slabs, LANES), modes,
     )
+    operands = [pltpu.with_memory_space_constraint(x, pltpu.HBM) for x in operands]
     return pl.pallas_call(
         functools.partial(exchange_kernel, n_grp, n_lev),
         out_shape=(
@@ -275,13 +268,12 @@
             jax.ShapeDtypeStruct((CORES, n_lev, piece, half), jnp.float32),
         ),
         in_specs=[hbm] * 5,
-        out_specs=(hbm, hbm),
+        out_specs=(vmem, vmem),
         scratch_shapes=[
             pltpu.VMEM(climatology.shape, jnp.float32),
             pltpu.VMEM((slabs, LANES), jnp.int32),
             pltpu.VMEM((slabs, LANES), jnp.int32),
             pltpu.VMEM(modes.shape, jnp.bfloat16),
-            pltpu.VMEM((width, col_dev), jnp.float32),
             pltpu.VMEM((n_lev, days, rows, LANES), jnp.bfloat16),
             pltpu.VMEM((n_lev, rows, LANES), jnp.float32),
             pltpu.VMEM((rows, LANES), jnp.int32),
@@ -295,7 +287,6 @@
             pltpu.VMEM((CORES, n_lev, piece, half), jnp.float32),
             pltpu.SemaphoreType.DMA((4,)),
             pltpu.SemaphoreType.DMA,
-            pltpu.SemaphoreType.DMA((3,)),
             pltpu.SemaphoreType.DMA((n_lev,)),
             pltpu.SemaphoreType.DMA((n_lev,)),
             pltpu.SemaphoreType.DMA((2, 2)),
@@ -362,19 +353,14 @@
     return jnp.concatenate(upper, axis=0), jnp.concatenate(inverse, axis=0)
 
 def whiten_kernel(
-    gram_hbm, stacked_hbm, factor_hbm, whitened_hbm,
-    pieces, gram_ref, stacked_ref, factor_ref, whitened_ref, sem,
+    pieces, stacked_ref, factor_hbm, whitened_hbm,
+    gram_ref, factor_ref, whitened_ref, sem,
 ):
     half = gram_ref.shape[1]
     long, short = half // pieces.shape[1], half // CORES // pieces.shape[1]
-    gram_in = pltpu.make_async_copy(gram_hbm, pieces, sem.at[0])
-    stacked_in = pltpu.make_async_copy(stacked_hbm, stacked_ref, sem.at[1])
-    first_out = pltpu.make_async_copy(whitened_ref.at[:half], whitened_hbm.at[:half], sem.at[2])
-    second_out = pltpu.make_async_copy(whitened_ref.at[half:], whitened_hbm.at[half:], sem.at[3])
-    factor_out = pltpu.make_async_copy(factor_ref, factor_hbm, sem.at[4])
-    gram_in.start()
-    stacked_in.start()
-    gram_in.wait()
+    first_out = pltpu.make_async_copy(whitened_ref.at[:half], whitened_hbm.at[:half], sem.at[0])
+    second_out = pltpu.make_async_copy(whitened_ref.at[half:], whitened_hbm.at[half:], sem.at[1])
+    factor_out = pltpu.make_async_copy(factor_ref, factor_hbm, sem.at[2])
     for c in range(CORES):
         for i in range(pieces.shape[1]):
             gram_ref[c, i * long : (i + 1) * long] = pieces[c, i, :long]
@@ -386,7 +372,6 @@
     factor_ref[:half, half:] = r12
     factor_ref[half:, :half] = jnp.zeros((half, half), jnp.float32)
     rest = gram_ref[2] - mm(r12, r12, ((0,), (0,)))
-    stacked_in.wait()
     first = mm(i11, stacked_ref[:half])
     whitened_ref[:half] = first
     first_out.start()
@@ -402,7 +387,7 @@
 
 
 def whiten(gram, stacked):
-    hbm = pl.BlockSpec(memory_space=pltpu.HBM)
+    vmem, hbm = pl.BlockSpec(memory_space=pltpu.VMEM), pl.BlockSpec(memory_space=pltpu.HBM)
     factor_shape = (stacked.shape[0],) * 2
     return pl.pallas_call(
         whiten_kernel,
@@ -410,15 +395,13 @@
             jax.ShapeDtypeStruct(factor_shape, jnp.float32),
             jax.ShapeDtypeStruct(stacked.shape, jnp.float32),
         ),
-        in_specs=[hbm, hbm],
+        in_specs=[vmem, vmem],
         out_specs=(hbm, hbm),
         scratch_shapes=[
-            pltpu.VMEM(gram.shape, jnp.float32),
             pltpu.VMEM((CORES + 1, gram.shape[3], gram.shape[3]), jnp.float32),
-            pltpu.VMEM(stacked.shape, jnp.float32),
             pltpu.VMEM(factor_shape, jnp.float32),
             pltpu.VMEM(stacked.shape, jnp.float32),
-            pltpu.SemaphoreType.DMA((5,)),
+            pltpu.SemaphoreType.DMA((3,)),
         ],
         compiler_params=pltpu.CompilerParams(vmem_limit_bytes=VMEM_BYTES),
         name="whiten",

time: 99.7 us -> 98.2 us (0.985)
  Pallas kernels: 98.9 us -> 97.3 us
    pallas_call x1, Pallas kernels: 11.3 us -> 10.2 us  [whiten(): pl.pallas_call(whiten_kernel, out_shape=(jax.ShapeDtypeStruct(factor_shap...]
where the time goes in v4:
time: 98.2 us; the launch traced here: 98 us
  Pallas kernels  97.3 us (99%)
    pallas_call x1, Pallas kernels, exchange(): pl.pallas_call(functools.partial(exchange_kernel, n_grp, n_lev), out_shap...  87.1 us
    pallas_call x1, Pallas kernels, whiten(): pl.pallas_call(whiten_kernel, out_shape=(jax.ShapeDtypeStruct(factor_shap...  10.2 us

profile of v4, /device:TPU:1, one launch (start us, length us, event | category | flops | bytes accessed | tf_op | source)
XLA Modules:
  0.0 98.0 jit_solution(8667029449638816539)
XLA Ops:
  0.6 87.1 %exchange.1 = (f32[256,1024]{1,0:T(8,128)S(1)}, f32[2,32,6,128]{3,2,1,0:T(8,128)S(1)}) custom-call(bf16[16,512,128]{2,1,0:T(8,128)(2,1)} %bitcast.7, f32[64,1024]{1,0:T(8,128)} %clim_hbm.1, s32[8,128]{1,0:T(8,128)} %bitcast.8, s32[8,128]{1,0:T(8,128)} %bitcast.9, bf16[16,64]{1,0:T(8,128)(2,1)} %modes_hbm.1), custom_call_target="tpu_custom_call" | custom-call | tf_op jit(solution)/shard_map/exchange/pallas_call | solution.py:264
  87.7 10.2 %whiten.1 = (f32[256,256]{1,0:T(8,128)}, f32[256,1024]{1,0:T(8,128)}) custom-call(f32[2,32,6,128]{3,2,1,0:T(8,128)S(1)} %get-tuple-element.4.pieces, f32[256,1024]{1,0:T(8,128)S(1)} %get-tuple-element.5.stacked_ref), custom_call_target="tpu_custom_call" | custom-call | tf_op jit(solution)/shard_map/whiten/pallas_call | solution.py:392

commit v5 on v4

--- a/solution.py
+++ b/solution.py
@@ -14,6 +14,8 @@
 VMEM_BYTES = 40 * 1024 * 1024
 CORES = 2
 N_X = 4
+SIDES = (1, -1)
+PARTS = 2
 
 
 def exchange_kernel(
@@ -21,8 +23,9 @@
     ocean_ref, clim_hbm, mask_hbm, bottom_hbm, modes_hbm,
     stacked_ref, gram_ref,
     clim_ref, mask_ref, bottom_ref, modes_ref,
-    recv, clim_rows, limit_rows, weights, anomaly, theirs, packed, pair_buf, rs_buf, sum_buf, gather_buf,
-    in_sem, local_sem, a_send, a_recv, p_sem, r_send, r_recv, s_send, s_recv, g_send, g_recv,
+    recv, clim_rows, limit_rows, weights, turned, anomaly, water_clim,
+    limit_out, limit_in, q_out, q_in, sums_out, sums_in, theirs, packed, pair_buf, rs_buf, sum_buf, gather_buf,
+    in_sem, local_sem, a_send, a_recv, l_sem, q_sem, t_sem, p_sem, r_send, r_recv, s_send, s_recv, g_send, g_recv,
 ):
     me_g = lax.axis_index("grp")
     me_l = lax.axis_index("lev")
@@ -47,18 +50,27 @@
 
     y_at = [lax.rem(me_l // N_X + d, n_y) * N_X for d in range(n_y)]
     x_at = [lax.rem(lax.rem(me_l, N_X) + d, N_X) for d in range(N_X)]
+
+    def at(dy, dx):
+        return y_at[dy % n_y] + x_at[dx % N_X]
+
     steps = [(dy, dx) for dy in far_first(n_y) for dx in far_first(N_X)][:-1]
-    peers = [y_at[dy] + x_at[dx] for dy, dx in steps]
-    senders = [y_at[-dy % n_y] + x_at[-dx % N_X] for dy, dx in steps]
-
-    def spiral(i, n):
-        half = (i + 1) // 2
-        return lax.rem(n // 2 + jnp.where(lax.rem(i, 2) == 1, half, n - half), n)
-
-    def sender(o):
-        y = lax.rem(me_l // N_X + spiral(o // N_X, n_y), n_y)
-        x = lax.rem(lax.rem(me_l, N_X) + spiral(lax.rem(o, N_X), N_X), N_X)
-        return y * N_X + x
+    peers = [at(dy, dx) for dy, dx in steps]
+    senders = [at(-dy, -dx) for dy, dx in steps]
+
+    reach = n_y // 2
+    first_k = N_X // 2
+    per_side = reach * N_X - first_k
+    routes = [(i, 0, dx, 0) for i, dx in enumerate(far_first(N_X))]
+    own_slots = len(routes)
+    side_routes = []
+    for k in range(first_k, reach * N_X):
+        hops = reach - 1 - k // N_X
+        for side, sign in enumerate(SIDES):
+            dx = k % N_X if side == 0 else N_X - 1 - k % N_X
+            slot = own_slots + side * per_side + k - first_k
+            side_routes.append((slot, sign * hops, dx, sign * (hops + 1)))
+    routes = side_routes + routes
 
     def z_to(o):
         return lax.rem(me_z + o, n_z)
@@ -80,34 +92,62 @@
     pl.semaphore_signal(barrier, inc=1, device_id=partner, device_id_type=MESH)
     pl.semaphore_wait(barrier, n_lev + n_z - 1)
 
-    def block_copy(to, slot, k):
+    part_days = DAYS // PARTS
+
+    def block_copy(part, owner, to, slot):
+        days = pl.ds(part * part_days, part_days)
         return pltpu.make_async_remote_copy(
-            src_ref=ocean_ref.at[:, pl.ds(pl.multiple_of(to * rows, rows), rows), :],
-            dst_ref=recv.at[slot],
-            send_sem=a_send.at[k],
-            recv_sem=a_recv.at[k],
+            src_ref=ocean_ref.at[days, pl.ds(pl.multiple_of(owner * rows, rows), rows), :],
+            dst_ref=recv.at[slot, days],
+            send_sem=a_send.at[part, slot],
+            recv_sem=a_recv.at[part, slot],
             device_id=(me_g, to),
             device_id_type=MESH,
         )
 
-    for o, peer in enumerate(peers):
-        block_copy(peer, me_l, o).start()
-
-    own = pltpu.make_async_copy(
-        ocean_ref.at[:, pl.ds(pl.multiple_of(me_l * rows, rows), rows), :], recv.at[me_l], local_sem
-    )
-    own.start()
+    def send_blocks(part):
+        for slot, hops, dx, dy in routes:
+            if (hops, dx) != (0, 0):
+                block_copy(part, at(dy, dx), at(hops, dx), slot).start()
+
+    stay = [
+        (slot, pltpu.make_async_copy(
+            ocean_ref.at[:, pl.ds(pl.multiple_of(at(dy, dx) * rows, rows), rows), :],
+            recv.at[slot], local_sem.at[i],
+        ))
+        for i, (slot, dy, dx) in enumerate(
+            [(slot, dy, dx) for slot, hops, dx, dy in routes if (hops, dx) == (0, 0)]
+        )
+    ]
+
+    send_blocks(0)
     for copy in inputs:
         copy.wait()
-
-    limit = jnp.where(mask_ref[...] == 1, bottom_ref[...], 0)
-    for slab in range(slabs):
-        limit_rows[2 * slab : 2 * slab + 1, :] = limit[slab : slab + 1, :]
-        limit_rows[2 * slab + 1 : 2 * slab + 2, :] = limit[slab : slab + 1, :] - 1
-
-    @pl.loop(0, clim_ref.shape[0] // 8)
-    def _(t):
-        block = clim_ref[pl.ds(pl.multiple_of(t * 8, 8), 8), :]
+    for _, copy in stay:
+        copy.start()
+
+    def neighbour_copy(src, dst, sems, sign):
+        return pltpu.make_async_remote_copy(
+            src_ref=src, dst_ref=dst, send_sem=sems.at[0], recv_sem=sems.at[1],
+            device_id=(me_g, at(sign, 0)), device_id_type=MESH,
+        )
+
+    limit_out[...] = jnp.where(mask_ref[...] == 1, bottom_ref[...], 0)
+    limit_copies = [
+        neighbour_copy(limit_out, limit_in.at[side], l_sem.at[side], -sign) for side, sign in enumerate(SIDES)
+    ]
+    for copy in limit_copies:
+        copy.start()
+
+    def spread_limit(limit, k):
+        for slab in range(slabs):
+            limit_rows[k, 2 * slab : 2 * slab + 1, :] = limit[slab : slab + 1, :]
+            limit_rows[k, 2 * slab + 1 : 2 * slab + 2, :] = limit[slab : slab + 1, :] - 1
+
+    spread_limit(limit_out[...], 2)
+
+    for t in range(clim_ref.shape[0] // 8):
+        block = clim_ref[8 * t : 8 * t + 8, :]
         for k in range(8):
             for slab in range(slabs):
                 row = 2 * slab + k % 2
@@ -118,41 +158,119 @@
     width = slabs * MODES
     depth = n_lev * rows
     levels = modes_ref.shape[1]
-    r = lax.broadcasted_iota(jnp.int32, (width, MODES), 0)
-    m = lax.broadcasted_iota(jnp.int32, (width, MODES), 1)
+    q = lax.broadcasted_iota(jnp.int32, (depth, levels), 0)
+    l = lax.broadcasted_iota(jnp.int32, (depth, levels), 1)
+    spread_levels = jnp.where(2 * (q // rows) + lax.rem(q, 2) == l, 1.0, 0.0).astype(jnp.bfloat16)
+    m = lax.broadcasted_iota(jnp.int32, (MODES, width), 0)
+    r = lax.broadcasted_iota(jnp.int32, (MODES, width), 1)
     spread_modes = jnp.where(lax.rem(r, MODES) == m, 1.0, 0.0).astype(jnp.bfloat16)
-    l = lax.broadcasted_iota(jnp.int32, (levels, depth), 0)
-    q = lax.broadcasted_iota(jnp.int32, (levels, depth), 1)
-    spread_levels = jnp.where(2 * (q // rows) + lax.rem(q, 2) == l, 1.0, 0.0).astype(jnp.bfloat16)
-    tall = jnp.dot(spread_modes, modes_ref[...], preferred_element_type=jnp.float32).astype(jnp.bfloat16)
-    wide = jnp.dot(tall, spread_levels, preferred_element_type=jnp.float32)
-    r = lax.broadcasted_iota(jnp.int32, (width, depth), 0)
-    q = lax.broadcasted_iota(jnp.int32, (width, depth), 1)
-    weights[...] = jnp.where(r // MODES == lax.rem(q, rows) // 2, wide, 0.0).astype(jnp.bfloat16)
-
-    def use(s):
-        water = limit_rows[...] > 2 * s
-        clim = clim_rows[s]
-        for d in range(DAYS):
-            diff = recv[s, d].astype(jnp.float32) - clim
-            anomaly[pl.ds(pl.multiple_of(s * rows, rows), rows), d * LANES : (d + 1) * LANES] = jnp.where(
-                water, diff, 0.0
+    tall = lax.dot_general(
+        spread_levels, modes_ref[...], (((1,), (1,)), ((), ())), preferred_element_type=jnp.float32
+    ).astype(jnp.bfloat16)
+    wide = jnp.dot(tall, spread_modes, preferred_element_type=jnp.float32)
+    q = lax.broadcasted_iota(jnp.int32, (depth, width), 0)
+    r = lax.broadcasted_iota(jnp.int32, (depth, width), 1)
+    wide = jnp.where(r // MODES == lax.rem(q, rows) // 2, wide, 0.0)
+    weights[...] = wide.astype(jnp.bfloat16)
+
+    for s in range(n_lev):
+        water_clim[s * rows : (s + 1) * rows] = jnp.where(limit_rows[2] > 2 * s, clim_rows[s], 0.0)
+    source = q // rows
+    dy = lax.rem(me_l // N_X + n_y - source // N_X, n_y)
+    dx = lax.rem(lax.rem(me_l, N_X) + N_X - lax.rem(source, N_X), N_X)
+    below = ((dy > 0) & (dy < reach)) | ((dy == reach) & (dx >= first_k))
+    above = (dy > reach) | ((dy == reach) & (dx < first_k))
+    q_copies = []
+    for side, sign in enumerate(SIDES):
+        q_out[side] = lax.dot_general(
+            jnp.where(above if side else below, wide, 0.0), water_clim[...], (((0,), (0,)), ((), ())),
+            precision=lax.Precision.HIGHEST, preferred_element_type=jnp.float32,
+        )
+        q_copies.append(neighbour_copy(q_out.at[side], q_in.at[side], q_sem.at[side], -sign))
+        q_copies[-1].start()
+
+    for part in range(1, PARTS):
+        send_blocks(part)
+
+    for slot, hops, dx, dy in routes:
+        s = at(-hops, -dx)
+        turned[slot * rows : (slot + 1) * rows] = weights[pl.ds(pl.multiple_of(s * rows, rows), rows)]
+
+    for copy in limit_copies:
+        copy.wait_recv()
+    for side in range(2):
+        spread_limit(limit_in[side], side)
+
+    def use(part, slot, s, kind):
+        water = limit_rows[kind] > 2 * s
+        for d in range(part * part_days, (part + 1) * part_days):
+            value = recv[slot, d].astype(jnp.float32)
+            if kind == 2:
+                value = value - clim_rows[s]
+            anomaly[pl.ds(pl.multiple_of(slot * rows, rows), rows), d * LANES : (d + 1) * LANES] = jnp.where(
+                water, value, 0.0
             ).astype(jnp.bfloat16)
 
-    own.wait()
-    use(me_l)
-
-    @pl.loop(0, n_lev - 1)
-    def _(o):
-        s = sender(o)
-        block_copy(s, s, o).wait_recv()
-        use(s)
-
-    coef = jnp.dot(weights[...], anomaly[...], preferred_element_type=jnp.float32)
+    def project(first, count, part, parts):
+        span = slice(first * rows, (first + count) * rows)
+        lanes = DAYS // parts * LANES
+        return lax.dot_general(
+            turned[span], anomaly[span, part * lanes : (part + 1) * lanes], (((0,), (0,)), ((), ())),
+            preferred_element_type=jnp.float32,
+        )
+
+    for _, copy in stay:
+        copy.wait()
+    at_home = [slot - own_slots - side * per_side for side, slot in enumerate(sorted(slot for slot, _ in stay)[1:])]
+    sum_copies = []
+    for part in range(PARTS):
+
+        @pl.loop(0, per_side)
+        def _(j):
+            k = j + first_k
+            hops, turn = reach - 1 - k // N_X, lax.rem(k, N_X)
+            for side, sign in enumerate(SIDES):
+                dx = turn if side == 0 else N_X - 1 - turn
+                y = lax.rem(me_l // N_X + n_y - sign * hops, n_y)
+                s = y * N_X + lax.rem(lax.rem(me_l, N_X) + N_X - dx, N_X)
+                slot = own_slots + side * per_side + j
+
+                @pl.when(j != at_home[side])
+                def _():
+                    block_copy(part, s, s, slot).wait_recv()
+
+                use(part, slot, s, side)
+
+        for side, sign in enumerate(SIDES):
+            if part == 0:
+                q_copies[side].wait_recv()
+            total = project(own_slots + side * per_side, per_side, part, PARTS)
+            for d in range(part_days):
+                sums_out[side, part, d] = (
+                    total[:, d * LANES : (d + 1) * LANES] - q_in[side]
+                ).astype(jnp.bfloat16)
+            sum_copies.append(
+                neighbour_copy(sums_out.at[side, part], sums_in.at[side, part], t_sem.at[side, part], sign)
+            )
+            sum_copies[-1].start()
+
+    for slot, hops, dx, dy in routes:
+        if slot < own_slots:
+            s = at(0, -dx)
+            for part in range(PARTS):
+                if dx:
+                    block_copy(part, s, s, slot).wait_recv()
+                use(part, slot, s, 2)
+    coef = project(0, own_slots, 0, 1)
+    for copy in sum_copies:
+        copy.wait_recv()
     for d in range(DAYS):
+        block = coef[:, d * LANES : (d + 1) * LANES]
+        for side in range(2):
+            block = block + sums_in[side, d // part_days, d % part_days].astype(jnp.float32)
         for slab in range(slabs):
-            stacked_ref[d * MODES : (d + 1) * MODES, slab * LANES : (slab + 1) * LANES] = coef[
-                slab * MODES : (slab + 1) * MODES, d * LANES : (d + 1) * LANES
+            stacked_ref[d * MODES : (d + 1) * MODES, slab * LANES : (slab + 1) * LANES] = block[
+                slab * MODES : (slab + 1) * MODES
             ]
 
     half = stacked_ref.shape[0] // 2
@@ -237,11 +355,16 @@
     to_pair.wait()
     gram_ref[1 - core] = gather_buf[1 - core]
     for o, peer in enumerate(peers):
-        block_copy(peer, me_l, o).wait_send()
         scatter_copy(peer, me_l, o).wait_send()
         gather_copy(peer, me_l, o).wait_send()
     for o in range(1, n_z):
         sum_copy(z_to(o), me_z, o).wait_send()
+    for part in range(PARTS):
+        for slot, hops, dx, dy in routes:
+            if (hops, dx) != (0, 0):
+                block_copy(part, at(dy, dx), at(hops, dx), slot).wait_send()
+    for copy in limit_copies + q_copies + sum_copies:
+        copy.wait_send()
 
 
 def exchange(n_grp, n_lev, ocean, climatology, land_mask, bottom_index, modes):
@@ -276,9 +399,17 @@
             pltpu.VMEM(modes.shape, jnp.bfloat16),
             pltpu.VMEM((n_lev, days, rows, LANES), jnp.bfloat16),
             pltpu.VMEM((n_lev, rows, LANES), jnp.float32),
-            pltpu.VMEM((rows, LANES), jnp.int32),
-            pltpu.VMEM((slabs * MODES, n_lev * rows), jnp.bfloat16),
+            pltpu.VMEM((3, rows, LANES), jnp.int32),
+            pltpu.VMEM((n_lev * rows, slabs * MODES), jnp.bfloat16),
+            pltpu.VMEM((n_lev * rows, slabs * MODES), jnp.bfloat16),
             pltpu.VMEM((n_lev * rows, days * LANES), jnp.bfloat16),
+            pltpu.VMEM((n_lev * rows, LANES), jnp.float32),
+            pltpu.VMEM((slabs, LANES), jnp.int32),
+            pltpu.VMEM((2, slabs, LANES), jnp.int32),
+            pltpu.VMEM((2, slabs * MODES, LANES), jnp.float32),
+            pltpu.VMEM((2, slabs * MODES, LANES), jnp.float32),
+            pltpu.VMEM((2, PARTS, days // PARTS, slabs * MODES, LANES), jnp.bfloat16),
+            pltpu.VMEM((2, PARTS, days // PARTS, slabs * MODES, LANES), jnp.bfloat16),
             pltpu.VMEM((n_lev, piece, half), jnp.float32),
             pltpu.VMEM((n_lev, piece, half), jnp.float32),
             pltpu.VMEM((n_lev, piece, half), jnp.float32),
@@ -286,9 +417,12 @@
             pltpu.VMEM((n_grp // CORES, piece, half), jnp.float32),
             pltpu.VMEM((CORES, n_lev, piece, half), jnp.float32),
             pltpu.SemaphoreType.DMA((4,)),
-            pltpu.SemaphoreType.DMA,
-            pltpu.SemaphoreType.DMA((n_lev,)),
-            pltpu.SemaphoreType.DMA((n_lev,)),
+            pltpu.SemaphoreType.DMA((3,)),
+            pltpu.SemaphoreType.DMA((PARTS, n_lev)),
+            pltpu.SemaphoreType.DMA((PARTS, n_lev)),
+            pltpu.SemaphoreType.DMA((2, 2)),
+            pltpu.SemaphoreType.DMA((2, 2)),
+            pltpu.SemaphoreType.DMA((2, PARTS, 2)),
             pltpu.SemaphoreType.DMA((2, 2)),
             pltpu.SemaphoreType.DMA((n_lev,)),
             pltpu.SemaphoreType.DMA((n_lev,)),

time: 98.2 us -> 90.1 us (0.918)
  Pallas kernels: 97.3 us -> 89.4 us
    pallas_call x1, Pallas kernels: 87.1 us -> 79.1 us  [exchange(): pl.pallas_call(functools.partial(exchange_kernel, n_grp, n_lev), out_shap...]
where the time goes in v5:
time: 90.1 us; the launch traced here: 90 us
  Pallas kernels  89.4 us (99%)
    pallas_call x1, Pallas kernels, exchange(): pl.pallas_call(functools.partial(exchange_kernel, n_grp, n_lev), out_shap...  79.1 us
    pallas_call x1, Pallas kernels, whiten(): pl.pallas_call(whiten_kernel, out_shape=(jax.ShapeDtypeStruct(factor_shap...  10.2 us

profile of v5, /device:TPU:1, one launch (start us, length us, event | category | flops | bytes accessed | tf_op | source)
XLA Modules:
  0.0 90.0 jit_solution(6958979640897329259)
XLA Ops:
  0.6 79.1 %exchange.1 = (f32[256,1024]{1,0:T(8,128)S(1)}, f32[2,32,6,128]{3,2,1,0:T(8,128)S(1)}) custom-call(bf16[16,512,128]{2,1,0:T(8,128)(2,1)} %bitcast.7, f32[64,1024]{1,0:T(8,128)} %clim_hbm.1, s32[8,128]{1,0:T(8,128)} %bitcast.8, s32[8,128]{1,0:T(8,128)} %bitcast.9, bf16[16,64]{1,0:T(8,128)(2,1)} %modes_hbm.1), custom_call_target="tpu_custom_call" | custom-call | tf_op jit(solution)/shard_map/exchange/pallas_call | solution.py:387
  79.8 10.2 %whiten.1 = (f32[256,256]{1,0:T(8,128)}, f32[256,1024]{1,0:T(8,128)}) custom-call(f32[2,32,6,128]{3,2,1,0:T(8,128)S(1)} %get-tuple-element.4.pieces, f32[256,1024]{1,0:T(8,128)S(1)} %get-tuple-element.5.stacked_ref), custom_call_target="tpu_custom_call" | custom-call | tf_op jit(solution)/shard_map/whiten/pallas_call | solution.py:526

commit v6 on v5

--- a/solution.py
+++ b/solution.py
@@ -262,6 +262,12 @@
                     block_copy(part, s, s, slot).wait_recv()
                 use(part, slot, s, 2)
     coef = project(0, own_slots, 0, 1)
+    for part in range(PARTS):
+        for slot, hops, dx, dy in routes:
+            if (hops, dx) != (0, 0):
+                block_copy(part, at(dy, dx), at(hops, dx), slot).wait_send()
+    for copy in limit_copies + q_copies + sum_copies:
+        copy.wait_send()
     for copy in sum_copies:
         copy.wait_recv()
     for d in range(DAYS):
@@ -330,6 +336,8 @@
 
     for o in range(1, n_z):
         sum_copy(z_to(o), me_z, o).start()
+    for o, peer in enumerate(peers):
+        scatter_copy(peer, me_l, o).wait_send()
     for o in range(1, n_z):
         s = z_from(o)
         sum_copy(s, s, o).wait_recv()
@@ -346,25 +354,18 @@
 
     for o, peer in enumerate(peers):
         gather_copy(peer, me_l, o).start()
+    for o in range(1, n_z):
+        sum_copy(z_to(o), me_z, o).wait_send()
     for o, s in enumerate(senders):
         gather_copy(s, s, o).wait_recv()
 
     to_pair = pair_copy(gather_buf.at[core], gather_buf.at[core], 1)
     to_pair.start()
     gram_ref[core] = gather_buf[core]
+    for o, peer in enumerate(peers):
+        gather_copy(peer, me_l, o).wait_send()
     to_pair.wait()
     gram_ref[1 - core] = gather_buf[1 - core]
-    for o, peer in enumerate(peers):
-        scatter_copy(peer, me_l, o).wait_send()
-        gather_copy(peer, me_l, o).wait_send()
-    for o in range(1, n_z):
-        sum_copy(z_to(o), me_z, o).wait_send()
-    for part in range(PARTS):
-        for slot, hops, dx, dy in routes:
-            if (hops, dx) != (0, 0):
-                block_copy(part, at(dy, dx), at(hops, dx), slot).wait_send()
-    for copy in limit_copies + q_copies + sum_copies:
-        copy.wait_send()
 
 
 def exchange(n_grp, n_lev, ocean, climatology, land_mask, bottom_index, modes):
@@ -493,8 +494,16 @@
     half = gram_ref.shape[1]
     long, short = half // pieces.shape[1], half // CORES // pieces.shape[1]
     first_out = pltpu.make_async_copy(whitened_ref.at[:half], whitened_hbm.at[:half], sem.at[0])
-    second_out = pltpu.make_async_copy(whitened_ref.at[half:], whitened_hbm.at[half:], sem.at[1])
-    factor_out = pltpu.make_async_copy(factor_ref, factor_hbm, sem.at[2])
+    cols = whitened_ref.shape[1] // 2
+    second_out = [
+        pltpu.make_async_copy(
+            whitened_ref.at[half:, i * cols : (i + 1) * cols],
+            whitened_hbm.at[half:, i * cols : (i + 1) * cols],
+            sem.at[1 + i],
+        )
+        for i in range(2)
+    ]
+    factor_out = pltpu.make_async_copy(factor_ref, factor_hbm, sem.at[3])
     for c in range(CORES):
         for i in range(pieces.shape[1]):
             gram_ref[c, i * long : (i + 1) * long] = pieces[c, i, :long]
@@ -513,11 +522,13 @@
     r22, i22 = eliminate(rest)
     factor_ref[half:, half:] = r22
     factor_out.start()
-    whitened_ref[half:] = mm(i22, left)
-    second_out.start()
+    for i in range(2):
+        whitened_ref[half:, i * cols : (i + 1) * cols] = mm(i22, left[:, i * cols : (i + 1) * cols])
+        second_out[i].start()
     first_out.wait()
     factor_out.wait()
-    second_out.wait()
+    for i in range(2):
+        second_out[i].wait()
 
 
 def whiten(gram, stacked):
@@ -535,7 +546,7 @@
             pltpu.VMEM((CORES + 1, gram.shape[3], gram.shape[3]), jnp.float32),
             pltpu.VMEM(factor_shape, jnp.float32),
             pltpu.VMEM(stacked.shape, jnp.float32),
-            pltpu.SemaphoreType.DMA((3,)),
+            pltpu.SemaphoreType.DMA((4,)),
         ],
         compiler_params=pltpu.CompilerParams(vmem_limit_bytes=VMEM_BYTES),
         name="whiten",

time: 90.1 us -> 89.8 us (level)
  no operation moved by 1% of the time
where the time goes in v6:
time: 89.8 us; the launch traced here: 89.7 us
  Pallas kernels  89.1 us (99%)
    pallas_call x1, Pallas kernels, exchange(): pl.pallas_call(functools.partial(exchange_kernel, n_grp, n_lev), out_shap...  78.9 us
    pallas_call x1, Pallas kernels, whiten(): pl.pallas_call(whiten_kernel, out_shape=(jax.ShapeDtypeStruct(factor_shap...  10.2 us

profile of v6, /device:TPU:1, one launch (start us, length us, event | category | flops | bytes accessed | tf_op | source)
XLA Modules:
  0.0 89.7 jit_solution(1156618033344930829)
XLA Ops:
  0.6 78.9 %exchange.1 = (f32[256,1024]{1,0:T(8,128)S(1)}, f32[2,32,6,128]{3,2,1,0:T(8,128)S(1)}) custom-call(bf16[16,512,128]{2,1,0:T(8,128)(2,1)} %bitcast.7, f32[64,1024]{1,0:T(8,128)} %clim_hbm.1, s32[8,128]{1,0:T(8,128)} %bitcast.8, s32[8,128]{1,0:T(8,128)} %bitcast.9, bf16[16,64]{1,0:T(8,128)(2,1)} %modes_hbm.1), custom_call_target="tpu_custom_call" | custom-call | tf_op jit(solution)/shard_map/exchange/pallas_call | solution.py:388
  79.6 10.2 %whiten.1 = (f32[256,256]{1,0:T(8,128)}, f32[256,1024]{1,0:T(8,128)}) custom-call(f32[2,32,6,128]{3,2,1,0:T(8,128)S(1)} %get-tuple-element.4.pieces, f32[256,1024]{1,0:T(8,128)S(1)} %get-tuple-element.5.stacked_ref), custom_call_target="tpu_custom_call" | custom-call | tf_op jit(solution)/shard_map/whiten/pallas_call | solution.py:537

commit v7 on v6

--- a/solution.py
+++ b/solution.py
@@ -266,18 +266,21 @@
         for slot, hops, dx, dy in routes:
             if (hops, dx) != (0, 0):
                 block_copy(part, at(dy, dx), at(hops, dx), slot).wait_send()
-    for copy in limit_copies + q_copies + sum_copies:
+    for copy in limit_copies + q_copies:
         copy.wait_send()
+    for part in range(PARTS):
+        for copy in sum_copies[2 * part : 2 * part + 2]:
+            copy.wait_recv()
+        for d in range(part * part_days, (part + 1) * part_days):
+            block = coef[:, d * LANES : (d + 1) * LANES]
+            for side in range(2):
+                block = block + sums_in[side, part, d % part_days].astype(jnp.float32)
+            for slab in range(slabs):
+                stacked_ref[d * MODES : (d + 1) * MODES, slab * LANES : (slab + 1) * LANES] = block[
+                    slab * MODES : (slab + 1) * MODES
+                ]
     for copy in sum_copies:
-        copy.wait_recv()
-    for d in range(DAYS):
-        block = coef[:, d * LANES : (d + 1) * LANES]
-        for side in range(2):
-            block = block + sums_in[side, d // part_days, d % part_days].astype(jnp.float32)
-        for slab in range(slabs):
-            stacked_ref[d * MODES : (d + 1) * MODES, slab * LANES : (slab + 1) * LANES] = block[
-                slab * MODES : (slab + 1) * MODES
-            ]
+        copy.wait_send()
 
     half = stacked_ref.shape[0] // 2
     share = half // CORES

time: 89.8 us -> 89.8 us (level)
  no operation moved by 1% of the time
where the time goes in v7:
time: 89.8 us; the launch traced here: 89.7 us
  Pallas kernels  89.1 us (99%)
    pallas_call x1, Pallas kernels, exchange(): pl.pallas_call(functools.partial(exchange_kernel, n_grp, n_lev), out_shap...  78.9 us
    pallas_call x1, Pallas kernels, whiten(): pl.pallas_call(whiten_kernel, out_shape=(jax.ShapeDtypeStruct(factor_shap...  10.2 us

profile of v7, /device:TPU:1, one launch (start us, length us, event | category | flops | bytes accessed | tf_op | source)
XLA Modules:
  0.0 89.7 jit_solution(15466659096506946447)
XLA Ops:
  0.6 78.9 %exchange.1 = (f32[256,1024]{1,0:T(8,128)S(1)}, f32[2,32,6,128]{3,2,1,0:T(8,128)S(1)}) custom-call(bf16[16,512,128]{2,1,0:T(8,128)(2,1)} %bitcast.7, f32[64,1024]{1,0:T(8,128)} %clim_hbm.1, s32[8,128]{1,0:T(8,128)} %bitcast.8, s32[8,128]{1,0:T(8,128)} %bitcast.9, bf16[16,64]{1,0:T(8,128)(2,1)} %modes_hbm.1), custom_call_target="tpu_custom_call" | custom-call | tf_op jit(solution)/shard_map/exchange/pallas_call | solution.py:391
  79.5 10.2 %whiten.1 = (f32[256,256]{1,0:T(8,128)}, f32[256,1024]{1,0:T(8,128)}) custom-call(f32[2,32,6,128]{3,2,1,0:T(8,128)S(1)} %get-tuple-element.4.pieces, f32[256,1024]{1,0:T(8,128)S(1)} %get-tuple-element.5.stacked_ref), custom_call_target="tpu_custom_call" | custom-call | tf_op jit(solution)/shard_map/whiten/pallas_call | solution.py:540
